TPU v7x, 128 devices: a whole 4x4x4 slice. The times are simulated.
128 devices in a mesh: seq: 64 (over z_hi, x, y, core), mp: 2 (over z_lo).
Axes of the slice: x: 4, y: 4, z: 4 (z_hi: 2, z_lo: 2; z = z_hi * 2 + z_lo), core: 2. Of those that a mesh axis runs over, the one named last changes fastest.
Arguments:
- clip_tokens: bfloat16 [512, 256, 768], P('seq'), may hold values from -6 to 6
- gain_spatial: float32 [768], replicated, may hold values from 0.5 to 1.5
- gain_temporal: float32 [768], replicated, may hold values from 0.5 to 1.5
- gain_mlp: float32 [768], replicated, may hold values from 0.5 to 1.5
- spatial_qkv: bfloat16 [768, 3, 768], P(None, None, 'mp'), may hold values from -0.21875 to 0.21875
- spatial_out: bfloat16 [768, 768], P('mp'), may hold values from -0.21875 to 0.21875
- temporal_qkv: bfloat16 [768, 3, 768], P(None, None, 'mp'), may hold values from -0.21875 to 0.21875
- temporal_out: bfloat16 [768, 768], P('mp'), may hold values from -0.21875 to 0.21875
- up_weight: bfloat16 [768, 3072], P(None, 'mp'), may hold values from -0.21875 to 0.21875
- down_weight: bfloat16 [3072, 768], P('mp'), may hold values from -0.109375 to 0.109375
Outputs:
- block_out: bfloat16 [512, 256, 768], P(('seq', 'mp'))
All inputs are finite; a program needn't handle non-finite values.
Results may differ from a plain program's by a relative error of at most 0.019.
Values may be sent and summed in bfloat16 or wider, within the bound.
A program may use at most 128 MiB of HBM per device.

v0:
```python
import jax
import jax.numpy as jnp
from jax import lax
from jax.sharding import PartitionSpec as P

HEAD_DIM = 64


def normalize(values, gain):
    values = values.astype(jnp.float32)
    center = values - jnp.mean(values, axis=-1, keepdims=True)
    spread = jnp.mean(center * center, axis=-1, keepdims=True)
    return (center * lax.rsqrt(spread + 1e-05) * gain).astype(jnp.bfloat16)


def attend(normed, w_qkv, w_out):
    batch, length, _ = normed.shape
    width = w_qkv.shape[2]
    heads = width // HEAD_DIM
    qkv = jnp.einsum("bld,dcw->blcw", normed, w_qkv, preferred_element_type=jnp.float32).astype(
        jnp.bfloat16
    )
    query = qkv[:, :, 0].reshape(batch, length, heads, HEAD_DIM)
    keys = qkv[:, :, 1].reshape(batch, length, heads, HEAD_DIM)
    vals = qkv[:, :, 2].reshape(batch, length, heads, HEAD_DIM)
    scores = jnp.einsum(
        "bqhe,bkhe->bhqk", query, keys, preferred_element_type=jnp.float32
    ) * HEAD_DIM ** (-0.5)
    weights = jnp.exp(scores)
    weights = (weights / jnp.sum(weights, axis=-1, keepdims=True)).astype(jnp.bfloat16)
    mixed = jnp.einsum("bhqk,bkhe->bqhe", weights, vals, preferred_element_type=jnp.float32).astype(
        jnp.bfloat16
    )
    mixed = mixed.reshape(batch, length, width)
    return jnp.einsum("blw,wd->bld", mixed, w_out, preferred_element_type=jnp.float32)


def per_device(
    clip_tokens,
    gain_spatial,
    gain_temporal,
    gain_mlp,
    spatial_qkv,
    spatial_out,
    temporal_qkv,
    temporal_out,
    up_weight,
    down_weight,
):
    frame_count, patch_count, width = clip_tokens.shape
    seq_count = lax.axis_size("seq")
    model_count = lax.axis_size("mp")
    model_index = lax.axis_index("mp")
    per_owner = patch_count // seq_count
    half_frames = frame_count // model_count
    partial_value = attend(normalize(clip_tokens, gain_spatial), spatial_qkv, spatial_out)
    total = lax.psum(partial_value.astype(jnp.bfloat16), "mp").astype(jnp.float32)
    spatial = (clip_tokens.astype(jnp.float32) + total).astype(jnp.bfloat16)
    positions = lax.all_to_all(spatial, "seq", split_axis=1, concat_axis=0, tiled=True)
    normed = jnp.swapaxes(normalize(positions, gain_temporal), 0, 1)
    temporal_part = jnp.swapaxes(attend(normed, temporal_qkv, temporal_out), 0, 1)
    temporal_total = lax.psum(temporal_part.astype(jnp.bfloat16), "mp").astype(jnp.float32)
    temporal = (positions.astype(jnp.float32) + temporal_total).astype(jnp.bfloat16)
    up = jnp.einsum(
        "fbd,dh->fbh", normalize(temporal, gain_mlp), up_weight, preferred_element_type=jnp.float32
    )
    hidden = jax.nn.gelu(up, approximate=False).astype(jnp.bfloat16)
    hidden_grid = hidden.reshape(seq_count, frame_count, per_owner, hidden.shape[-1])
    mlp_part = lax.psum_scatter(
        jnp.einsum(
            "nfbh,hd->fnbd", hidden_grid, down_weight, preferred_element_type=jnp.float32
        ).astype(jnp.bfloat16),
        "mp",
        scatter_dimension=0,
        tiled=True,
    ).astype(jnp.float32)
    temporal_grid = temporal.reshape(seq_count, frame_count, per_owner, width)
    own_rows = jnp.swapaxes(
        lax.dynamic_slice_in_dim(temporal_grid, model_index * half_frames, half_frames, 1), 0, 1
    )
    finished = (own_rows.astype(jnp.float32) + mlp_part).astype(jnp.bfloat16)
    returned = lax.all_to_all(finished, "seq", split_axis=1, concat_axis=2, tiled=True)
    return returned.reshape(half_frames, patch_count, width)


def solution(mesh):
    return jax.shard_map(
        per_device,
        mesh=mesh,
        in_specs=(
            P("seq", None, None),
            P(),
            P(),
            P(),
            P(None, None, "mp"),
            P("mp", None),
            P(None, None, "mp"),
            P("mp", None),
            P(None, "mp"),
            P("mp", None),
        ),
        out_specs=P(("seq", "mp"), None, None),
        check_vma=False,
    )
```

profile of v0, /device:TPU:1, one launch (start us, length us, event | category | flops | bytes accessed | tf_op | source)
XLA Modules:
  0.0 475.3 jit_solution(11953381208464028547)
XLA Ops:
  9.1 3.0 fusion.17
  12.1 4.9 %fusion.49 = bf16[8,256,3,384]{3,1,2,0:T(8,128)(2,1)S(1)} fusion(bf16[8,256,768]{2,1,0:T(8,128)(2,1)S(1)} %copy-done.3, f32[768]{0:T(1024)S(1)} %copy-done.10, f32[8,256]{1,0:T(8,128)S(1)} %add_rsqrt_fusion.2, f32[8,256]{1,0:T(8,128)S(1)} %broadcast_multiply_fusion.2, bf16[768,3,384]{2,0,1:T(8,128)(2,1)S(1)} %copy-done.7), kind=kOutput, calls=%fused_computation.71 | convolution fusion | flops 3634102272 | bytes 9653248 | tf_op jit(solution)/shard_map/bld,dcw->blcw/dot_general | solution.py:20
  19.3 2.6 copy.91
  21.9 2.6 copy.92
  24.5 2.6 copy.93
  27.1 4.4 fusion.12
  34.0 3.5 convolution_convert_fusion
  37.6 95.8 %all-reduce.3.cloned.1.call-done = bf16[8,256,768]{2,1,0:T(8,128)(2,1)} async-done(((bf16[8,256,768]{2,1,0:T(8,128)(2,1)}), bf16[8,256,768]{2,1,0:T(8,128)(2,1)}) %all-reduce.3.cloned.1.call-update) | async-done | bytes 3145744 | tf_op jit(solution)/shard_map/psum | solution.py:57
  133.4 3.6 fusion.23
  138.8 51.2 %all_to_all.8 = bf16[8,256,768]{2,0,1:T(8,128)(2,1)S(1)} all-to-all(bf16[8,256,768]{2,0,1:T(8,128)(2,1)S(1)} %copy.96), channel_id=1, replica_groups=mesh['seq'=64,'mp'=2] {'seq'}, dimensions={1} | all-to-all | bytes 6291456 | tf_op jit(solution)/shard_map/all_to_all | solution.py:59
  190.9 5.1 %copy.141 = f32[8,64,4,768]{3,2,1,0:T(4,128)} copy(f32[8,64,4,768]{3,0,2,1:T(8,128)S(1)} %bitcast_convert_fusion) | data formatting | bytes 12582912 | tf_op jit(solution)/shard_map/convert_element_type | solution.py:63
  199.0 9.7 %multiply_reduce_fusion = f32[64,8,4]{2,0,1:T(8,128)S(1)} fusion(f32[64,8,4]{2,0,1:T(8,128)S(1)} %copy.101, f32[8,64,4,768]{3,0,2,1:T(8,128)} %copy-done.2), kind=kLoop, calls=%fused_computation.51 | loop fusion | flops 4716544 | bytes 6307840 | tf_op jit(solution)/shard_map/reduce_sum | solution.py:12
  209.2 9.6 %fusion.52 = bf16[4,512,3,384]{1,3,2,0:T(8,128)(2,1)S(1)} fusion(f32[64,8,4,768]{3,2,0,1:T(4,128)} %bitcast.101, f32[768]{0:T(1024)S(1)} %copy-done.11, f32[512,4]{0,1:T(4,128)S(1)} %rsqrt.29, f32[512,4]{0,1:T(4,128)S(1)} %div.41, bf16[768,3,384]{2,0,1:T(8,128)(2,1)} %param.16), kind=kOutput, calls=%fused_computation.72 | convolution fusion | flops 3632529408 | bytes 12798976 | tf_op jit(solution)/shard_map/bld,dcw->blcw/dot_general | solution.py:20
  219.1 10.7 %fusion = (f32[4,6,512]{2,1,0:T(8,128)S(1)}, f32[4,6,512,512]{2,3,1,0:T(8,128)}) fusion(bf16[4,512,6,64]{1,3,2,0:T(8,128)(2,1)S(1)} %bitcast.105, bf16[4,512,6,64]{1,3,2,0:T(8,128)(2,1)S(1)} %bitcast.104), kind=kOutput, calls=%fused_computation.2 | convolution fusion | flops 817876992 | bytes 28360704 | tf_op jit(solution)/shard_map/bqhe,bkhe->bhqk/dot_general | solution.py:26
  229.8 10.9 %fusion.63 = bf16[4,6,64,512]{3,2,1,0:T(8,128)(2,1)S(1)} fusion(bf16[4,512,6,64]{1,3,2,0:T(8,128)(2,1)S(1)} %bitcast.109, f32[4,6,512,512]{2,3,1,0:T(8,128)} %get-tuple-element.16, f32[4,6,512]{2,1,0:T(8,128)S(1)} %get-tuple-element.15), kind=kOutput, calls=%fused_computation.78 | convolution fusion | flops 824967168 | bytes 28360704 | tf_op jit(solution)/shard_map/bhqk,bkhe->bqhe/dot_general | solution.py:31
  240.7 3.6 convert_bitcast_fusion.1
  244.3 88.7 %all-reduce.5.cloned.1.call-done = bf16[512,4,768]{2,0,1:T(8,128)(2,1)} async-done(((bf16[512,4,768]{2,0,1:T(8,128)(2,1)}), bf16[512,4,768]{2,0,1:T(8,128)(2,1)}) %all-reduce.5.cloned.1.call-update) | async-done | bytes 3145744 | tf_op jit(solution)/shard_map/psum | solution.py:62
  333.0 7.3 %convert_reduce_fusion.1 = (f32[512,4]{0,1:T(4,128)S(1)}, bf16[512,4,768]{2,0,1:T(8,128)(2,1)S(1)}) fusion(bf16[512,4,768]{2,0,1:T(8,128)(2,1)} %all-reduce.5.cloned.1.call-done, f32[64,8,4,768]{3,2,0,1:T(4,128)} %bitcast.102), kind=kLoop, calls=%fused_computation.30 | loop fusion | flops 7862272 | bytes 12591104 | tf_op jit(solution)/shard_map/reduce_sum | solution.py:11
  341.4 31.8 %fusion.31 = bf16[64,8,4,1536]{3,1,0,2:T(8,128)(2,1)S(1)} fusion(bf16[512,4,768]{2,0,1:T(8,128)(2,1)S(1)} %get-tuple-element.6, f32[768]{0:T(1024)S(1)} %copy-done.12, f32[512,4]{0,1:T(4,128)S(1)} %add_rsqrt_fusion.1, f32[512,4]{0,1:T(4,128)S(1)} %broadcast_multiply_fusion.1, bf16[768,1536]{1,0:T(8,128)(2,1)S(1)} %copy-done), kind=kOutput, calls=%fused_computation.53 | convolution fusion | flops 5044174848 | bytes 11815936 | tf_op jit(solution)/shard_map/fbd,dh->fbh/dot_general | solution.py:64
  373.3 5.3 %convert_bitcast_fusion = bf16[8,64,4,768]{3,0,2,1:T(8,128)(2,1)S(1)} fusion(bf16[1536,768]{1,0:T(8,128)(2,1)S(1)} %copy-done.6, bf16[64,8,4,1536]{3,1,0,2:T(8,128)(2,1)S(1)} %fusion.31), kind=kOutput, calls=%fused_computation.60 | convolution fusion | flops 4833411072 | bytes 11796480 | tf_op jit(solution)/shard_map/nfbh,hd->fnbd/dot_general | solution.py:70
  378.6 3.4 copy.109
  382.0 3.8 constant_dynamic-slice_fusion
  385.9 43.2 %reduce-scatter.2.cloned.1.call-done = bf16[4,64,4,768]{3,1,2,0:T(8,128)(2,1)} async-done(((bf16[8,64,4,768]{3,1,2,0:T(8,128)(2,1)}), bf16[4,64,4,768]{3,1,2,0:T(8,128)(2,1)}) %reduce-scatter.2.cloned.1.call-update) | async-done | bytes 1572880 | tf_op jit(solution)/shard_map/reduce_scatter | solution.py:69
  432.7 33.9 %all_to_all.9 = bf16[4,64,4,768]{3,2,0,1:T(4,128)(2,1)S(1)} all-to-all(bf16[4,64,4,768]{3,2,0,1:T(4,128)(2,1)S(1)} %copy.110), channel_id=1, replica_groups=mesh['seq'=64,'mp'=2] {'seq'}, dimensions={1} | all-to-all | bytes 3145728 | tf_op jit(solution)/shard_map/all_to_all | solution.py:82
  (57 shorter events, 20.4 us)
Async XLA Ops:
  6.5 334.9 %copy-start = (bf16[768,1536]{1,0:T(8,128)(2,1)S(1)}, bf16[768,1536]{1,0:T(8,128)(2,1)}, u32[]{:S(2)}) copy-start(bf16[768,1536]{1,0:T(8,128)(2,1)} %param.18) | copy-start | bytes 7077892
  6.5 5.5 %copy-start.10 = (f32[768]{0:T(1024)S(1)}, f32[768]{0:T(1024)}, u32[]{:S(2)}) copy-start(f32[768]{0:T(1024)} %param.11) | copy-start | bytes 9220
  6.5 126.9 %all-reduce.3.cloned.1.call-start = ((), (), s32[]{:S(2)}) async-start(), calls=%async_computation.3 | async-start | bytes 6291456 | tf_op jit(solution)/shard_map/psum | solution.py:57
  6.5 5.5 %copy-start.3 = (bf16[8,256,768]{2,1,0:T(8,128)(2,1)S(1)}, bf16[8,256,768]{2,1,0:T(8,128)(2,1)}, u32[]{:S(2)}) copy-start(bf16[8,256,768]{2,1,0:T(8,128)(2,1)} %param.10) | copy-start | bytes 9437188
  6.5 5.5 %copy-start.7 = (bf16[768,3,384]{2,0,1:T(8,128)(2,1)S(1)}, bf16[768,3,384]{2,0,1:T(8,128)(2,1)}, u32[]{:S(2)}) copy-start(bf16[768,3,384]{2,0,1:T(8,128)(2,1)} %param.14) | copy-start | bytes 5308420
  27.1 4.4 copy-start.5
  31.5 2.5 copy-start.8
  37.6 295.4 %all-reduce.5.cloned.1.call-start = ((), (), s32[]{:S(2)}) async-start(), calls=%async_computation.4 | async-start | bytes 6291456 | tf_op jit(solution)/shard_map/psum | solution.py:62
  190.9 5.2 %copy-start.2 = (f32[8,64,4,768]{3,0,2,1:T(8,128)}, f32[8,64,4,768]{3,0,2,1:T(8,128)S(1)}, u32[]{:S(2)}) copy-start(f32[8,64,4,768]{3,0,2,1:T(8,128)S(1)} %bitcast_convert_fusion) | copy-start | bytes 18874372
  196.0 13.1 %copy-start.11 = (f32[768]{0:T(1024)S(1)}, f32[768]{0:T(1024)}, u32[]{:S(2)}) copy-start(f32[768]{0:T(1024)} %param.12) | copy-start | bytes 9220
  229.8 10.9 %copy-start.9 = (bf16[384,768]{1,0:T(8,128)(2,1)S(1)}, bf16[384,768]{1,0:T(8,128)(2,1)}, u32[]{:S(2)}) copy-start(bf16[384,768]{1,0:T(8,128)(2,1)} %param.17) | copy-start | bytes 1769476
  244.3 97.1 %copy-start.12 = (f32[768]{0:T(1024)S(1)}, f32[768]{0:T(1024)}, u32[]{:S(2)}) copy-start(f32[768]{0:T(1024)} %param.13) | copy-start | bytes 9220
  244.3 184.8 %reduce-scatter.2.cloned.1.call-start = ((), (), s32[]{:S(2)}) async-start(), calls=%async_computation.5 | async-start | bytes 4718592 | tf_op jit(solution)/shard_map/reduce_scatter | solution.py:69
  340.3 33.0 %copy-start.4 = (bf16[512,4,768]{2,0,1:T(8,128)(2,1)}, bf16[512,4,768]{2,0,1:T(8,128)(2,1)S(1)}, u32[]{:S(2)}) copy-start(bf16[512,4,768]{2,0,1:T(8,128)(2,1)S(1)} %get-tuple-element.6) | copy-start | bytes 9437188
  341.4 31.9 %copy-start.6 = (bf16[1536,768]{1,0:T(8,128)(2,1)S(1)}, bf16[1536,768]{1,0:T(8,128)(2,1)}, u32[]{:S(2)}) copy-start(bf16[1536,768]{1,0:T(8,128)(2,1)} %param.19) | copy-start | bytes 7077892
  429.1 39.4 %copy-start.1 = (bf16[768,1536]{1,0:T(8,128)(2,1)S(1)}, bf16[768,1536]{1,0:T(8,128)(2,1)}, u32[]{:S(2)}) copy-start(bf16[768,1536]{1,0:T(8,128)(2,1)} %param.18) | copy-start | bytes 7077892
Sparse Core Ops, SparseCore 0:
  37.7 95.7 all-reduce.2
  244.4 88.5 all-reduce.4
  382.1 46.8 reduce-scatter.1
where the time goes:
time: 484 us; the launch traced here: 475 us
  waiting for transfers between devices  228 us (47%)
  matrix products  87.2 us (18%)
  blocking collectives  85.1 us (18%)
  other arithmetic  32.9 us (7%)
  local copies, waits for them, and re-layouts  28.6 us (6%)
  between operations  13.6 us (3%)
    psum x1, waiting for transfers between devices, per_device(): lax.psum(partial_value.astype(jnp.bfloat16), 'mp').astype(jnp.float32)  95.8 us
    psum x1, waiting for transfers between devices, per_device(): lax.psum(temporal_part.astype(jnp.bfloat16), 'mp').astype(jnp.float32)  88.7 us
    all_to_all x1, blocking collectives, per_device(): lax.all_to_all(spatial, 'seq', split_axis=1, concat_axis=0, tiled=True)  51.2 us
    reduce_scatter x1, waiting for transfers between devices, per_device(): lax.psum_scatter(jnp.einsum('nfbh,hd->fnbd', hidden_grid, down_weight, pr...  43.2 us
    all_to_all x1, blocking collectives, per_device(): lax.all_to_all(finished, 'seq', split_axis=1, concat_axis=2, tiled=True)  33.9 us
    dot_general x1, matrix products, per_device(): jnp.einsum('fbd,dh->fbh', normalize(temporal, gain_mlp), up_weight, prefe...  31.8 us
    dot_general x2, matrix products, attend(): jnp.einsum('bqhe,bkhe->bhqk', query, keys, preferred_element_type=jnp.flo...  15.1 us
    dot_general x2, matrix products, attend(): jnp.einsum('bld,dcw->blcw', normed, w_qkv, preferred_element_type=jnp.flo...  14.5 us
  transfers between devices with their start and end apart: 3, of which 3 were waited for; matrix products, arithmetic and copies ran while one was open for 1% of the time, Pallas kernels for 0%

commit v1 on v0

--- a/solution.py
+++ b/solution.py
@@ -48,39 +48,30 @@
     down_weight,
 ):
     frame_count, patch_count, width = clip_tokens.shape
-    seq_count = lax.axis_size("seq")
     model_count = lax.axis_size("mp")
     model_index = lax.axis_index("mp")
-    per_owner = patch_count // seq_count
     half_frames = frame_count // model_count
-    partial_value = attend(normalize(clip_tokens, gain_spatial), spatial_qkv, spatial_out)
-    total = lax.psum(partial_value.astype(jnp.bfloat16), "mp").astype(jnp.float32)
-    spatial = (clip_tokens.astype(jnp.float32) + total).astype(jnp.bfloat16)
-    positions = lax.all_to_all(spatial, "seq", split_axis=1, concat_axis=0, tiled=True)
-    normed = jnp.swapaxes(normalize(positions, gain_temporal), 0, 1)
-    temporal_part = jnp.swapaxes(attend(normed, temporal_qkv, temporal_out), 0, 1)
-    temporal_total = lax.psum(temporal_part.astype(jnp.bfloat16), "mp").astype(jnp.float32)
-    temporal = (positions.astype(jnp.float32) + temporal_total).astype(jnp.bfloat16)
+
+    def whole(weight, axis):
+        return lax.all_gather(weight, "mp", axis=axis, tiled=True)
+
+    spatial_qkv, spatial_out = whole(spatial_qkv, 2), whole(spatial_out, 0)
+    temporal_qkv, temporal_out = whole(temporal_qkv, 2), whole(temporal_out, 0)
+    up_weight, down_weight = whole(up_weight, 1), whole(down_weight, 0)
+    own = lax.dynamic_slice_in_dim(clip_tokens, model_index * half_frames, half_frames, 0)
+    mixed = attend(normalize(own, gain_spatial), spatial_qkv, spatial_out)
+    spatial = (own.astype(jnp.float32) + mixed).astype(jnp.bfloat16)
+    positions = lax.all_to_all(spatial, ("seq", "mp"), split_axis=1, concat_axis=0, tiled=True)
+    positions = jnp.swapaxes(positions, 0, 1)
+    mixed = attend(normalize(positions, gain_temporal), temporal_qkv, temporal_out)
+    temporal = (positions.astype(jnp.float32) + mixed).astype(jnp.bfloat16)
     up = jnp.einsum(
-        "fbd,dh->fbh", normalize(temporal, gain_mlp), up_weight, preferred_element_type=jnp.float32
+        "bfd,dh->bfh", normalize(temporal, gain_mlp), up_weight, preferred_element_type=jnp.float32
     )
     hidden = jax.nn.gelu(up, approximate=False).astype(jnp.bfloat16)
-    hidden_grid = hidden.reshape(seq_count, frame_count, per_owner, hidden.shape[-1])
-    mlp_part = lax.psum_scatter(
-        jnp.einsum(
-            "nfbh,hd->fnbd", hidden_grid, down_weight, preferred_element_type=jnp.float32
-        ).astype(jnp.bfloat16),
-        "mp",
-        scatter_dimension=0,
-        tiled=True,
-    ).astype(jnp.float32)
-    temporal_grid = temporal.reshape(seq_count, frame_count, per_owner, width)
-    own_rows = jnp.swapaxes(
-        lax.dynamic_slice_in_dim(temporal_grid, model_index * half_frames, half_frames, 1), 0, 1
-    )
-    finished = (own_rows.astype(jnp.float32) + mlp_part).astype(jnp.bfloat16)
-    returned = lax.all_to_all(finished, "seq", split_axis=1, concat_axis=2, tiled=True)
-    return returned.reshape(half_frames, patch_count, width)
+    down = jnp.einsum("bfh,hd->bfd", hidden, down_weight, preferred_element_type=jnp.float32)
+    finished = jnp.swapaxes((temporal.astype(jnp.float32) + down).astype(jnp.bfloat16), 0, 1)
+    return lax.all_to_all(finished, ("seq", "mp"), split_axis=0, concat_axis=1, tiled=True)
 
 
 def solution(mesh):

time: 484 us -> 417 us (0.86)
  blocking collectives: 85.1 us -> 33.5 us
  other arithmetic: 32.9 us -> 4.49 us
  waiting for transfers between devices: 228 us -> 203 us
  matrix products: 87.2 us -> 105 us
  local copies, waits for them, and re-layouts: 28.6 us -> 39.4 us
  starting transfers between devices: 0.09 us -> 9.45 us
    psum x2 -> x0, waiting for transfers between devices: 184 us -> none  [the longest x1 95.8 us: per_device(): lax.psum(partial_value.astype(jnp.bfloat16), 'mp').astype(jnp.float32)]
    all_gather x0 -> x6, waiting for transfers between devices: none -> 176 us  [whole(): return lax.all_gather(weight, 'mp', axis=axis, tiled=True)]
    all_to_all x2 -> x1, blocking collectives: 85.1 us -> 33.5 us  [per_device(): lax.all_to_all(finished, ('seq', 'mp'), split_axis=0, concat_axis=1, tile...]
    reduce_scatter x1 -> x0, waiting for transfers between devices: 43.2 us -> none  [per_device(): lax.psum_scatter(jnp.einsum('nfbh,hd->fnbd', hidden_grid, down_weight, pr...]
    all_to_all x0 -> x1, waiting for transfers between devices: none -> 23.9 us  [per_device(): lax.all_to_all(spatial, ('seq', 'mp'), split_axis=1, concat_axis=0, tiled...]
    dot_general x2, matrix products: 37.1 us -> 53.6 us  [the longest x1 36.8 us: per_device(): jnp.einsum('bfh,hd->bfd', hidden, down_weight, preferred_element_type=jnp...]
    reduce_sum x3, other arithmetic: 13.7 us -> 1.66 us  [normalize(): spread = jnp.mean(center * center, axis=-1, keepdims=True)]
    reduce_sum x3 -> x2, other arithmetic: 12.3 us -> 0.51 us  [normalize(): center = values - jnp.mean(values, axis=-1, keepdims=True)]
  transfers between devices with their start and end apart: 3 -> 7, of which waited for: 3 -> 6; matrix products, arithmetic and copies ran while one was open for 1% -> 26% of each run, Pallas kernels for 0% -> 0%
where the time goes in v1:
time: 417 us; the launch traced here: 409 us
  waiting for transfers between devices  203 us (49%)
  matrix products  105 us (25%)
  local copies, waits for them, and re-layouts  39.4 us (9%)
  blocking collectives  33.5 us (8%)
  between operations  14 us (3%)
  starting transfers between devices  9.45 us (2%)
  other arithmetic  4.49 us (1%)
    all_gather x6, waiting for transfers between devices, whole(): return lax.all_gather(weight, 'mp', axis=axis, tiled=True)  176 us
    dot_general x1, matrix products, per_device(): jnp.einsum('bfh,hd->bfd', hidden, down_weight, preferred_element_type=jnp...  36.8 us
    all_to_all x1, blocking collectives, per_device(): lax.all_to_all(finished, ('seq', 'mp'), split_axis=0, concat_axis=1, tile...  33.5 us
    all_to_all x1, waiting for transfers between devices, per_device(): lax.all_to_all(spatial, ('seq', 'mp'), split_axis=1, concat_axis=0, tiled...  23.9 us
    dot_general x1, matrix products, per_device(): jnp.einsum('bfd,dh->bfh', normalize(temporal, gain_mlp), up_weight, prefe...  16.8 us
    dot_general x2, matrix products, attend(): jnp.einsum('bhqk,bkhe->bqhe', weights, vals, preferred_element_type=jnp.f...  15.1 us
    dot_general x2, matrix products, attend(): jnp.einsum('bqhe,bkhe->bhqk', query, keys, preferred_element_type=jnp.flo...  15 us
    convert_element_type x1, local copies, waits for them, and re-layouts, per_device(): temporal = (positions.astype(jnp.float32) + mixed).astype(jnp.bfloat16)  14.5 us
  transfers between devices with their start and end apart: 7, of which 6 were waited for; matrix products, arithmetic and copies ran while one was open for 26% of the time, Pallas kernels for 0%

profile of v1, /device:TPU:1, one launch (start us, length us, event | category | flops | bytes accessed | tf_op | source)
XLA Modules:
  0.0 408.9 jit_solution(8281949848811715907)
XLA Ops:
  10.8 53.4 %all-gather.7.cloned.1.call-done = bf16[768,3,768]{2,0,1:T(8,128)(2,1)} async-done(((bf16[768,3,384]{2,0,1:T(8,128)(2,1)}), bf16[768,3,768]{2,0,1:T(8,128)(2,1)}) %all-gather.7.cloned.1.call-update) | async-done | bytes 3538960 | tf_op jit(solution)/shard_map/all_gather | solution.py:56
  64.2 6.3 %fusion.38 = bf16[4,256,3,768]{3,1,2,0:T(8,128)(2,1)S(1)} fusion(bf16[768,3,768]{2,0,1:T(8,128)(2,1)} %all-gather.7.cloned.1.call-done, f32[768]{0:T(1024)S(1)} %copy-done.5, f32[4,256]{1,0:T(4,128)S(1)} %add_rsqrt_fusion.2, f32[4,256]{1,0:T(4,128)S(1)} %broadcast_multiply_fusion.2, bf16[8,256,768]{2,1,0:T(8,128)(2,1)S(1)} %copy-done.1, s32[]{:T(128)S(6)} %select_n.3), kind=kOutput, calls=%fused_computation.67 | convolution fusion | flops 3630170112 | bytes 9842692 | tf_op jit(solution)/shard_map/bld,dcw->blcw/dot_general | solution.py:20
  74.9 2.6 copy.35
  77.5 2.6 fusion.11
  80.2 3.3 fusion.49
  83.5 8.7 %all-gather.9.cloned.1.call-done = bf16[768,768]{1,0:T(8,128)(2,1)} async-done(((bf16[384,768]{1,0:T(8,128)(2,1)}), bf16[768,768]{1,0:T(8,128)(2,1)}) %all-gather.9.cloned.1.call-update) | async-done | bytes 1179664 | tf_op jit(solution)/shard_map/all_gather | solution.py:56
  92.3 3.2 fusion.32
  95.4 2.4 copy.40
  97.8 9.3 %all-to-all-start = ((bf16[4,256,768]{2,0,1:T(4,128)(2,1)}), bf16[4,256,768]{2,0,1:T(4,128)(2,1)S(1)}, u32[]{:S(2)}, u32[]{:S(2)}) async-start(bf16[4,256,768]{2,0,1:T(4,128)(2,1)} %copy.40), calls=%async_computation | async-start | bytes 3145728 | tf_op jit(solution)/shard_map/all_to_all | solution.py:64
  107.6 23.9 %all-to-all-done = bf16[4,256,768]{2,0,1:T(4,128)(2,1)S(1)} async-done(((bf16[4,256,768]{2,0,1:T(4,128)(2,1)}), bf16[4,256,768]{2,0,1:T(4,128)(2,1)S(1)}, u32[]{:S(2)}, u32[]{:S(2)}) %all-to-all-start) | async-done | bytes 1572896 | tf_op jit(solution)/shard_map/all_to_all | solution.py:64
  133.8 14.5 %reshape.57 = f32[512,2,768]{2,0,1:T(8,128)S(1)} reshape(f32[128,4,2,768]{3,1,0,2:T(4,128)} %copy_bitcast_fusion) | data formatting | bytes 6291456 | tf_op jit(solution)/shard_map/convert_element_type | solution.py:67
  149.1 14.7 %all-gather.11.cloned.1.call-done = bf16[768,3,768]{2,0,1:T(8,128)(2,1)} async-done(((bf16[768,3,384]{2,0,1:T(8,128)(2,1)}), bf16[768,3,768]{2,0,1:T(8,128)(2,1)}) %all-gather.11.cloned.1.call-update) | async-done | bytes 3538960 | tf_op jit(solution)/shard_map/all_gather | solution.py:56
  163.7 6.2 %fusion.41 = bf16[2,512,3,768]{3,1,2,0:T(8,128)(2,1)S(1)} fusion(bf16[768,3,768]{2,0,1:T(8,128)(2,1)} %all-gather.11.cloned.1.call-done, f32[512,2,768]{2,0,1:T(8,128)S(1)} %reshape.57, f32[768]{0:T(1024)S(1)} %copy-done.6, f32[2,512]{1,0:T(2,128)S(1)} %add_rsqrt_fusion.1, f32[2,512]{1,0:T(2,128)S(1)} %broadcast_multiply_fusion.1), kind=kOutput, calls=%fused_computation.68 | convolution fusion | flops 3629383680 | bytes 11414528 | tf_op jit(solution)/shard_map/bld,dcw->blcw/dot_general | solution.py:20
  172.3 2.6 copy.43
  174.9 2.7 copy.44
  177.6 2.6 copy.42
  180.1 12.4 %fusion = (f32[2,12,512]{2,1,0:T(8,128)S(1)}, f32[2,12,512,512]{2,3,1,0:T(8,128)}) fusion(bf16[2,512,12,64]{1,3,2,0:T(8,128)(2,1)} %bitcast.93, bf16[2,512,12,64]{1,3,2,0:T(8,128)(2,1)} %bitcast.94), kind=kOutput, calls=%fused_computation.2 | convolution fusion | flops 817876992 | bytes 28360704 | tf_op jit(solution)/shard_map/bqhe,bkhe->bhqk/dot_general | solution.py:26
  192.5 11.8 %fusion.48 = bf16[2,12,64,512]{3,2,1,0:T(8,128)(2,1)} fusion(bf16[2,512,12,64]{1,3,2,0:T(8,128)(2,1)S(1)} %bitcast.99, f32[2,12,512,512]{2,3,1,0:T(8,128)} %get-tuple-element.18, f32[2,12,512]{2,1,0:T(8,128)S(1)} %get-tuple-element.17), kind=kOutput, calls=%fused_computation.69 | convolution fusion | flops 824967168 | bytes 28360704 | tf_op jit(solution)/shard_map/bhqk,bkhe->bqhe/dot_general | solution.py:31
  204.3 5.3 %convert_reduce_fusion.1 = (f32[2,512]{1,0:T(2,128)S(1)}, bf16[2,512,768]{2,1,0:T(8,128)(2,1)S(1)}, f32[2,512,768]{2,1,0:T(8,128)}) fusion(f32[512,2,768]{2,0,1:T(8,128)S(1)} %reshape.57, bf16[2,512,768]{1,2,0:T(8,128)(2,1)} %bitcast.97, bf16[768,768]{1,0:T(8,128)(2,1)} %all-gather.13.cloned.1.call-done), kind=kOutput, calls=%fused_computation.38 | convolution fusion | flops 1211104256 | bytes 10620928 | tf_op jit(solution)/shard_map/blw,wd->bld/dot_general | solution.py:35
  211.4 48.0 %all-gather.15.cloned.1.call-done = bf16[768,3072]{1,0:T(8,128)(2,1)} async-done(((bf16[768,1536]{1,0:T(8,128)(2,1)}), bf16[768,3072]{1,0:T(8,128)(2,1)}) %all-gather.15.cloned.1.call-update) | async-done | bytes 4718608 | tf_op jit(solution)/shard_map/all_gather | solution.py:56
  259.4 16.8 %fusion.37 = (u8[512,3072]{1,0:T(8,128)(4,1)}, u8[512,3072]{1,0:T(8,128)(4,1)}, f32[2,512,3072]{2,1,0:T(8,128)}) fusion(bf16[768,3072]{1,0:T(8,128)(2,1)} %all-gather.15.cloned.1.call-done, bf16[2,512,768]{2,1,0:T(8,128)(2,1)} %copy-done, f32[768]{0:T(1024)S(1)} %copy-done.7, f32[2,512]{1,0:T(2,128)S(1)} %add_rsqrt_fusion, ...), kind=kOutput, calls=%fused_computation.66 | convolution fusion | flops 4873519104 | bytes 22031360 | tf_op jit(solution)/shard_map/bfd,dh->bfh/dot_general | solution.py:68
  276.2 50.9 %all-gather.17.cloned.1.call-done = bf16[3072,768]{1,0:T(8,128)(2,1)} async-done(((bf16[1536,768]{1,0:T(8,128)(2,1)}), bf16[3072,768]{1,0:T(8,128)(2,1)}) %all-gather.17.cloned.1.call-update) | async-done | bytes 4718608 | tf_op jit(solution)/shard_map/all_gather | solution.py:56
  327.1 36.8 %fusion.33 = bf16[512,2,768]{2,0,1:T(8,128)(2,1)S(1)} fusion(bf16[3072,768]{1,0:T(8,128)(2,1)} %all-gather.17.cloned.1.call-done, f32[2,512,3072]{2,1,0:T(8,128)} %get-tuple-element.20, f32[512,2,768]{2,0,1:T(8,128)S(1)} %reshape.57, f32[2,512,768]{2,1,0:T(8,128)} %get-tuple-element.19, u8[512,3072]{1,0:T(8,128)(4,1)} %get-tuple-element.6, ...), kind=kOutput, calls=%fused_computation.55 | convolution fusion | flops 5055971328 | bytes 28311552 | tf_op jit(solution)/shard_map/bfh,hd->bfd/dot_general | solution.py:72
  365.5 33.5 %all_to_all.27 = bf16[512,2,768]{2,1,0:T(2,128)(2,1)S(1)} all-to-all(bf16[512,2,768]{2,1,0:T(2,128)(2,1)S(1)} %copy.47), channel_id=1, replica_groups=mesh['seq'=64,'mp'=2] {'seq','mp'}, dimensions={0} | all-to-all | bytes 3145728 | tf_op jit(solution)/shard_map/all_to_all | solution.py:74
  (48 shorter events, 20.4 us)
Async XLA Ops:
  6.5 3.4 copy-start.1
  6.5 57.7 %all-gather.7.cloned.1.call-start = ((), (), s32[]{:S(2)}) async-start(), calls=%async_computation.2 | async-start | bytes 5308416 | tf_op jit(solution)/shard_map/all_gather | solution.py:56
  7.3 85.0 %all-gather.9.cloned.1.call-start = ((), (), s32[]{:S(2)}) async-start(), calls=%async_computation.3 | async-start | bytes 1769472 | tf_op jit(solution)/shard_map/all_gather | solution.py:56
  8.0 56.2 %copy-start.5 = (f32[768]{0:T(1024)S(1)}, f32[768]{0:T(1024)}, u32[]{:S(2)}) copy-start(f32[768]{0:T(1024)} %param.11) | copy-start | bytes 9220
  8.0 155.7 %all-gather.11.cloned.1.call-start = ((), (), s32[]{:S(2)}) async-start(), calls=%async_computation.4 | async-start | bytes 5308416 | tf_op jit(solution)/shard_map/all_gather | solution.py:56
  8.8 195.6 %all-gather.13.cloned.1.call-start = ((), (), s32[]{:S(2)}) async-start(), calls=%async_computation.5 | async-start | bytes 1769472 | tf_op jit(solution)/shard_map/all_gather | solution.py:56
  9.3 250.0 %all-gather.15.cloned.1.call-start = ((), (), s32[]{:S(2)}) async-start(), calls=%async_computation.6 | async-start | bytes 7077888 | tf_op jit(solution)/shard_map/all_gather | solution.py:56
  77.5 2.6 copy-start.3
  80.2 12.1 %copy-start.2 = (bf16[8,256,768]{2,1,0:T(8,128)(2,1)S(1)}, bf16[8,256,768]{2,1,0:T(8,128)(2,1)}, u32[]{:S(2)}) copy-start(bf16[8,256,768]{2,1,0:T(8,128)(2,1)} %param.10) | copy-start | bytes 9437188
  97.8 33.8 %all-to-all-start = ((bf16[4,256,768]{2,0,1:T(4,128)(2,1)}), bf16[4,256,768]{2,0,1:T(4,128)(2,1)S(1)}, u32[]{:S(2)}, u32[]{:S(2)}) async-start(bf16[4,256,768]{2,0,1:T(4,128)(2,1)} %copy.40), calls=%async_computation | async-start | bytes 3145728 | tf_op jit(solution)/shard_map/all_to_all | solution.py:64
  107.0 220.1 %all-gather.17.cloned.1.call-start = ((), (), s32[]{:S(2)}) async-start(), calls=%async_computation.7 | async-start | bytes 7077888 | tf_op jit(solution)/shard_map/all_gather | solution.py:56
  148.3 15.4 %copy-start.6 = (f32[768]{0:T(1024)S(1)}, f32[768]{0:T(1024)}, u32[]{:S(2)}) copy-start(f32[768]{0:T(1024)} %param.12) | copy-start | bytes 9220
  180.1 12.4 %copy-start.4 = (bf16[2,512,1,768]{1,3,0,2:T(8,128)(2,1)S(1)}, bf16[2,512,1,768]{1,3,0,2:T(8,128)(2,1)}, u32[]{:S(2)}) copy-start(bf16[2,512,1,768]{1,3,0,2:T(8,128)(2,1)} %copy.42) | copy-start | bytes 4718596
  204.3 55.1 %copy-start.7 = (f32[768]{0:T(1024)S(1)}, f32[768]{0:T(1024)}, u32[]{:S(2)}) copy-start(f32[768]{0:T(1024)} %param.13) | copy-start | bytes 9220
  209.6 1.1 copy-start
Sparse Core Ops, SparseCore 0:
  9.0 55.1 all-gather.6
  65.9 26.3 all-gather.8
  93.9 69.7 all-gather.10
  165.2 26.3 all-gather.12
  193.1 66.2 all-gather.14
  260.9 66.2 all-gather.16

commit v2 on v1

v2 whole, which is shorter than its diff:
```python
import functools
import math

import jax
import jax.numpy as jnp
from jax import lax
from jax.experimental import pallas as pl
from jax.experimental.pallas import tpu as pltpu
from jax.sharding import PartitionSpec as P

MESH = pl.DeviceIdType.MESH
F32, BF16 = jnp.float32, jnp.bfloat16
HEAD_DIM = 64
D = 768
HALF = 384
TOKENS = 256
DEVICES = 128
GROUP = 32
Q_SCALE = math.log2(math.e) * HEAD_DIM**-0.5
ROWS = (768, 384, 768, 384, 768, 1536)
STACKED = (False, True, False, True, False, True)


def dot(a, b):
    return jnp.dot(a, b, preferred_element_type=F32)


def layer_norm(values, gain):
    values = values.astype(F32)
    center = values - jnp.mean(values, axis=-1, keepdims=True)
    spread = jnp.mean(center * center, axis=-1, keepdims=True)
    return (center * lax.rsqrt(spread + 1e-05) * gain).astype(BF16)


def attend_pair(query, keys, vals):
    first = lax.broadcasted_iota(jnp.int32, (1, 128), 1) < HEAD_DIM
    zero = jnp.zeros_like(query)
    one = jnp.ones_like(vals)
    outs = []
    for mine in (first, jnp.logical_not(first)):
        scores = lax.dot_general(
            jnp.where(mine, query, zero), keys, (((1,), (1,)), ((), ())), preferred_element_type=F32
        )
        weights = jnp.exp2(scores).astype(BF16)
        filled = jnp.where(mine, vals, one)
        both = jnp.concatenate([filled * BF16(2.0**-8), filled * BF16(2.0**24)], axis=1)
        outs.append(dot(weights, both))
    out_a, out_b = outs
    low_top, low_sum = jnp.where(first, out_a[:, :128], out_b[:, :128]), jnp.where(
        first, out_b[:, :128], out_a[:, :128]
    )
    high_top, high_sum = jnp.where(first, out_a[:, 128:], out_b[:, 128:]), jnp.where(
        first, out_b[:, 128:], out_a[:, 128:]
    )
    low_sum = pltpu.roll(low_sum, HEAD_DIM, 1)
    high_sum = pltpu.roll(high_sum, HEAD_DIM, 1)
    large = low_sum > 2.0**-8
    return (jnp.where(large, low_top, high_top) / jnp.where(large, low_sum, high_sum)).astype(BF16)


def gelu(value):
    return 0.5 * value * (1.0 + lax.erf(value * 0.5**0.5))


def bits(index, *fields):
    total = jnp.zeros_like(index)
    for shift, width, to in fields:
        total = total + (((index >> shift) & ((1 << width) - 1)) << to)
    return total


def one_hot(*fields):
    row = lax.broadcasted_iota(jnp.int32, (512, 512), 0)
    column = lax.broadcasted_iota(jnp.int32, (512, 512), 1)
    return jnp.where(bits(row, *fields) == column, 1.0, 0.0).astype(BF16)


def kernel(
    clip, gain_s, gain_t, gain_m, w0, w1, w2, w3, w4, w5, out,
    x, normed, qkv_s, qkv_t, mixed, positions,
    send1, recv1, send2, recv2, perm,
    f0, f1, f2, f3, f4, f5,
    x_sem, own_sem, z_send, z_recv, core_send, core_recv, round_sem,
    a_send, a_recv, b_send, b_recv,
):
    s, m = lax.axis_index("seq"), lax.axis_index("mp")
    me = s * 2 + m
    group, place = me // GROUP, lax.rem(me, GROUP)
    z_hi, core = s // 32, lax.rem(s, 2)
    owned = (w0, w1, w2, w3, w4, w5)
    full = (f0, f1, f2, f3, f4, f5)

    def part(k, half, start, rows):
        if STACKED[k]:
            return full[k].at[pl.ds(pl.multiple_of(half * ROWS[k] + start, 16), rows)]
        return full[k].at[half, pl.ds(pl.multiple_of(start, 16), rows)]

    def flip(bit):
        return me + bit * (1 - 2 * lax.rem(me // bit, 2))

    def device(index):
        return (index // 2, lax.rem(index, 2))

    def load(k):
        return pltpu.make_async_copy(owned[k], part(k, m, 0, ROWS[k]), own_sem.at[k])

    def z_start(k):
        rows = ROWS[k] // 4
        start = (z_hi * 2 + core) * rows
        for other in range(2):
            pltpu.make_async_remote_copy(
                src_ref=owned[k].at[pl.ds(pl.multiple_of(start, 16), rows)],
                dst_ref=part(k, m, start, rows),
                send_sem=z_send.at[k],
                recv_sem=z_recv.at[k, z_hi],
                device_id=(other * 32 + lax.rem(s, 32), 1 - m),
                device_id_type=MESH,
            ).start()

    def z_forward(k):
        rows = ROWS[k] // 4
        for source in range(2):
            piece = part(k, 1 - m, (source * 2 + core) * rows, rows)
            pltpu.make_async_copy(piece, piece, z_recv.at[k, source]).wait()
            pltpu.make_async_remote_copy(
                src_ref=piece,
                dst_ref=piece,
                send_sem=core_send.at[k],
                recv_sem=core_recv.at[k],
                device_id=device(flip(2)),
                device_id_type=MESH,
            ).start()

    def half_bytes(k, sem):
        block = part(k, 0, 0, ROWS[k] // 2)
        pltpu.make_async_copy(block, block, sem.at[k]).wait()

    def z_finish(k):
        half_bytes(k, core_recv)

    def exchange(b, to, send, recv, send_sem, recv_sem):
        @pl.when(b == 0)
        def _():
            own = pl.ds(pl.multiple_of(me * 16, 16), 16)
            pltpu.make_async_copy(send.at[own], recv.at[own], recv_sem.at[group]).start()

        def step(i, carry):
            dest = to * GROUP + lax.rem(i + place, GROUP)
            pltpu.make_async_remote_copy(
                src_ref=send.at[pl.ds(pl.multiple_of(dest * 16, 16), 16)],
                dst_ref=recv.at[pl.ds(pl.multiple_of(me * 16, 16), 16)],
                send_sem=send_sem,
                recv_sem=recv_sem.at[group],
                device_id=device(dest),
                device_id_type=MESH,
            ).start()
            return carry

        lax.fori_loop(jnp.where(b == 0, 1, 0), GROUP, step, 0)

    def arrived(recv, recv_sem, source):
        block = recv.at[pl.ds(pl.multiple_of(source * 512, 512), 512)]
        pltpu.make_async_copy(block, block, recv_sem.at[source]).wait()
        return block[...]

    barrier = pltpu.get_barrier_semaphore()
    for bit in (1, 2, 4, 8, 16, 32, 64):
        pl.semaphore_signal(barrier, inc=1, device_id=device(flip(bit)), device_id_type=MESH)
    pl.semaphore_signal(
        barrier, inc=1, device_id=(lax.rem(s + 32, 64), 1 - m), device_id_type=MESH
    )
    own_frames = pltpu.make_async_copy(clip.at[pl.ds(m * 4, 4)], x, x_sem)
    own_frames.start()
    for k in range(6):
        load(k).start()
    perm[0] = one_hot((4, 5, 1), (3, 1, 8), (2, 1, 0), (0, 2, 6))
    perm[1] = one_hot((8, 1, 3), (7, 1, 2), (2, 5, 4), (0, 2, 0))
    perm[2] = one_hot((4, 5, 2), (3, 1, 8), (2, 1, 7), (0, 2, 0))
    perm[3] = one_hot((8, 1, 3), (6, 2, 0), (1, 5, 4), (0, 1, 2))
    own_frames.wait()

    @pl.loop(0, 4)
    def _(f):
        normed[pl.ds(pl.multiple_of(f * TOKENS, TOKENS), TOKENS)] = layer_norm(x[f], gain_s[...])

    pl.semaphore_wait(barrier, 8)
    z_start(0)
    z_start(1)

    columns = lax.broadcasted_iota(jnp.int32, (1, 3 * HALF), 1)
    scale = jnp.where(columns < HALF, Q_SCALE, 1.0).astype(F32)

    def spatial_heads(half):
        @pl.loop(0, 4)
        def _(f):
            rows = pl.ds(pl.multiple_of(f * TOKENS, TOKENS), TOKENS)
            qkv_s[rows] = (dot(normed[rows], f0[half]) * scale).astype(BF16)

        @pl.loop(0, 4)
        def _(f):
            rows = pl.ds(pl.multiple_of(f * TOKENS, TOKENS), TOKENS)
            for pair in range(3):
                c = pair * 128
                mixed[rows, pl.ds(pl.multiple_of(half * HALF + c, 128), 128)] = attend_pair(
                    qkv_s[rows, c : c + 128],
                    qkv_s[rows, HALF + c : HALF + c + 128],
                    qkv_s[rows, 2 * HALF + c : 2 * HALF + c + 128],
                )

    load(0).wait()
    spatial_heads(m)
    for r in range(7):
        pl.semaphore_signal(
            round_sem.at[r], inc=1, device_id=device(flip(1 << r)), device_id_type=MESH
        )
        pl.semaphore_wait(round_sem.at[r], 1)
    z_forward(0)
    z_forward(1)
    z_start(2)
    z_start(3)
    z_finish(0)
    spatial_heads(1 - m)
    load(1).wait()
    z_finish(1)

    @pl.loop(0, 4)
    def _(f):
        rows = pl.ds(pl.multiple_of(f * TOKENS, TOKENS), TOKENS)
        x[f] = (x[f].astype(F32) + dot(mixed[rows], f1[...])).astype(BF16)

    @pl.loop(0, 4)
    def _(b):
        to = lax.rem(group + b, 4)
        rows = pl.ds(pl.multiple_of(to * 64, 64), 64)
        block = jnp.concatenate(
            [x[f, rows, h * HALF : (h + 1) * HALF] for h in range(2) for f in range(4)], axis=0
        )
        send1[pl.ds(pl.multiple_of(to * 512, 512), 512)] = dot(perm[0], block).astype(BF16)
        exchange(b, to, send1, recv1, a_send, a_recv)

    z_start(4)
    z_start(5)
    z_forward(2)
    z_forward(3)
    load(2).wait()
    z_finish(2)

    @pl.loop(0, 4)
    def _(b):
        source = lax.rem(group + 4 - b, 4)
        block = dot(perm[1], arrived(recv1, a_recv, source)).astype(BF16)
        tokens = jnp.concatenate([block[:TOKENS], block[TOKENS:]], axis=1)
        normal = layer_norm(tokens, gain_t[...])
        for p in range(2):
            rows = pl.ds(pl.multiple_of(p * 512 + b * 128, 128), 128)
            positions[rows] = tokens[p * 128 : (p + 1) * 128]
        for half in range(2):
            made = (dot(normal, f2[half]) * scale).astype(BF16)
            for p in range(2):
                qkv_t[half, pl.ds(pl.multiple_of(p * 512 + b * 128, 128), 128)] = made[
                    p * 128 : (p + 1) * 128
                ]

    for p in range(2):

        @pl.loop(0, 4)
        def _(t):
            half = t // 2
            every = slice(p * 512, (p + 1) * 512)
            rows = pl.ds(pl.multiple_of(p * 512 + lax.rem(t, 2) * TOKENS, TOKENS), TOKENS)
            for pair in range(3):
                c = pair * 128
                mixed[rows, pl.ds(pl.multiple_of(half * HALF + c, 128), 128)] = attend_pair(
                    qkv_t[half, rows, c : c + 128],
                    qkv_t[half, every, HALF + c : HALF + c + 128],
                    qkv_t[half, every, 2 * HALF + c : 2 * HALF + c + 128],
                )

        z_forward(4 + p)

    load(3).wait()
    z_finish(3)
    load(4).wait()
    z_finish(4)
    load(5).wait()
    z_finish(5)

    @pl.loop(0, 4)
    def _(b):
        rows = [pl.ds(pl.multiple_of(p * 512 + b * 128, 128), 128) for p in range(2)]
        total = dot(jnp.concatenate([mixed[r] for r in rows], axis=0), f3[...])
        tokens = jnp.concatenate([positions[r] for r in rows], axis=0)
        tokens = (tokens.astype(F32) + total).astype(BF16)
        normal = layer_norm(tokens, gain_m[...])
        total = tokens.astype(F32)
        for j in range(4):
            up = dot(normal, f4[j // 2, :, (j % 2) * D : (j % 2 + 1) * D])
            total = total + dot(gelu(up).astype(BF16), f5[j * D : (j + 1) * D])
        done = total.astype(BF16)
        block = jnp.concatenate([done[:, :HALF], done[:, HALF:]], axis=0)
        to = lax.rem(group + 4 - b, 4)
        send2[pl.ds(pl.multiple_of(to * 512, 512), 512)] = dot(perm[2], block).astype(BF16)
        exchange(b, to, send2, recv2, b_send, b_recv)

    @pl.loop(0, 4)
    def _(b):
        source = lax.rem(group + b, 4)
        block = dot(perm[3], arrived(recv2, b_recv, source)).astype(BF16)
        rows = pl.ds(pl.multiple_of(source * 64, 64), 64)
        for h in range(2):
            for f in range(4):
                at = h * TOKENS + f * 64
                out[f, rows, h * HALF : (h + 1) * HALF] = block[at : at + 64]

    for send, sem in ((send1, a_send), (send2, b_send)):
        sent = send.at[pl.ds(0, (DEVICES - 1) * 16)]
        pltpu.make_async_copy(sent, sent, sem).wait()
    for k in range(6):
        half_bytes(k, z_send)
        half_bytes(k, core_send)


def per_device(clip, gain_s, gain_t, gain_m, w0, w1, w2, w3, w4, w5):
    w0, w2 = w0.reshape(D, 3 * HALF), w2.reshape(D, 3 * HALF)
    gains = [g.reshape(1, D) for g in (gain_s, gain_t, gain_m)]
    vmem, anywhere = pl.BlockSpec(memory_space=pltpu.VMEM), pl.BlockSpec(memory_space=pl.ANY)
    dma = pltpu.SemaphoreType.DMA
    return pl.pallas_call(
        kernel,
        out_shape=jax.ShapeDtypeStruct((4, 256, D), BF16),
        in_specs=[anywhere, vmem, vmem, vmem] + [anywhere] * 6,
        out_specs=vmem,
        scratch_shapes=[
            pltpu.VMEM((4, 256, D), BF16),
            pltpu.VMEM((1024, D), BF16),
            pltpu.VMEM((1024, 3 * HALF), BF16),
            pltpu.VMEM((2, 1024, 3 * HALF), BF16),
            pltpu.VMEM((1024, D), BF16),
            pltpu.VMEM((1024, D), BF16),
            pltpu.VMEM((2048, HALF), BF16),
            pltpu.VMEM((2048, HALF), BF16),
            pltpu.VMEM((2048, HALF), BF16),
            pltpu.VMEM((2048, HALF), BF16),
            pltpu.VMEM((4, 512, 512), BF16),
            pltpu.VMEM((2, D, 3 * HALF), BF16),
            pltpu.VMEM((D, D), BF16),
            pltpu.VMEM((2, D, 3 * HALF), BF16),
            pltpu.VMEM((D, D), BF16),
            pltpu.VMEM((2, D, 1536), BF16),
            pltpu.VMEM((3072, D), BF16),
            dma,
            dma((6,)),
            dma((6,)),
            dma((6, 2)),
            dma((6,)),
            dma((6,)),
            pltpu.SemaphoreType.REGULAR((7,)),
            dma,
            dma((4,)),
            dma,
            dma((4,)),
        ],
        compiler_params=pltpu.CompilerParams(
            collective_id=0, has_side_effects=True, vmem_limit_bytes=60 << 20
        ),
        cost_estimate=pl.CostEstimate(
            flops=22 * 10**9, bytes_accessed=13 * 10**6, transcendentals=12 * 10**6
        ),
    )(clip, *gains, w0, w1, w2, w3, w4, w5)


def solution(mesh):
    return jax.shard_map(
        per_device,
        mesh=mesh,
        in_specs=(
            P("seq", None, None),
            P(),
            P(),
            P(),
            P(None, None, "mp"),
            P("mp", None),
            P(None, None, "mp"),
            P("mp", None),
            P(None, "mp"),
            P("mp", None),
        ),
        out_specs=P(("seq", "mp"), None, None),
        check_vma=False,
    )
```

time: 417 us -> 133 us (0.32); the launches traced: 409 us -> 133 us
  waiting for transfers between devices: 203 us -> 0 us
  Pallas kernels: 0 us -> 120 us
  matrix products: 105 us -> 0 us
  blocking collectives: 33.5 us -> 0 us
  local copies, waits for them, and re-layouts: 39.4 us -> 12.5 us
  between operations: 14 us -> 0.06 us
  starting transfers between devices: 9.45 us -> 0 us
  other arithmetic: 4.49 us -> 0 us
    all_gather x6 -> x0, waiting for transfers between devices: 176 us -> none  [whole(): return lax.all_gather(weight, 'mp', axis=axis, tiled=True)]
    pallas_call x0 -> x1, Pallas kernels: none -> 120 us  [per_device(): pl.pallas_call(kernel, out_shape=jax.ShapeDtypeStruct((4, 256, D), BF16),...]
    dot_general x10 -> x0, matrix products: 105 us -> none  [the longest x1 36.8 us: per_device(): jnp.einsum('bfh,hd->bfd', hidden, down_weight, preferred_element_type=jnp...]
    all_to_all x1 -> x0, blocking collectives: 33.5 us -> none  [per_device(): lax.all_to_all(finished, ('seq', 'mp'), split_axis=0, concat_axis=1, tile...]
    all_to_all x1 -> x0, waiting for transfers between devices: 23.9 us -> none  [per_device(): lax.all_to_all(spatial, ('seq', 'mp'), split_axis=1, concat_axis=0, tiled...]
    convert_element_type x3 -> x0, local copies, waits for them, and re-layouts: 18.5 us -> none  [the longest x1 14.5 us: per_device(): temporal = (positions.astype(jnp.float32) + mixed).astype(jnp.bfloat16)]
    slice x8 -> x0, local copies, waits for them, and re-layouts: 17.2 us -> none  [the longest x4 8.7 us: attend(): keys = qkv[:, :, 1].reshape(batch, length, heads, HEAD_DIM)]
    all_to_all x1 -> x0, starting transfers between devices: 9.26 us -> none  [per_device(): lax.all_to_all(spatial, ('seq', 'mp'), split_axis=1, concat_axis=0, tiled...]
  transfers between devices with their start and end apart: 7 -> 0, of which waited for: 6 -> 0; matrix products, arithmetic and copies ran while one was open for 26% -> 0% of each run, Pallas kernels for 0% -> 0%
where the time goes in v2:
time: 133 us
  Pallas kernels  120 us (90%)
  local copies, waits for them, and re-layouts  12.5 us (9%)
    pallas_call x1, Pallas kernels, per_device(): pl.pallas_call(kernel, out_shape=jax.ShapeDtypeStruct((4, 256, D), BF16),...  120 us
    unnamed x11, local copies, waits for them, and re-layouts  6.24 us
    reshape x2, local copies, waits for them, and re-layouts, per_device(): w0, w2 = (w0.reshape(D, 3 * HALF), w2.reshape(D, 3 * HALF))  4.5 us

profile of v2, /device:TPU:1, one launch (start us, length us, event | category | flops | bytes accessed | tf_op | source)
XLA Modules:
  0.0 133.0 jit_solution(13713053008409686508)
XLA Ops:
  0.0 2.6 %copy.13 = bf16[768,3,384]{0,2,1:T(8,128)(2,1)S(1)} copy(bf16[768,3,384]{2,0,1:T(8,128)(2,1)} %param.14) | data formatting | bytes 3538944 | tf_op args[4]
  2.6 0.0 copy-start
  2.6 2.3 %copy.15.w0 = bf16[768,1152]{1,0:T(8,128)(2,1)} copy(bf16[768,1152]{0,1:T(8,128)(2,1)S(1)} %bitcast.2) | data formatting | bytes 3538944 | tf_op jit(solution)/shard_map/reshape | solution.py:324
  4.9 0.0 copy-done
  4.9 0.9 copy.14
  5.8 0.0 copy-start.1
  5.9 0.0 copy-start.2
  5.9 0.0 copy-start.3
  5.9 2.2 %copy.16.w2 = bf16[768,1152]{1,0:T(8,128)(2,1)} copy(bf16[768,1152]{0,1:T(8,128)(2,1)S(1)} %bitcast.3) | data formatting | bytes 3538944 | tf_op jit(solution)/shard_map/reshape | solution.py:324
  8.1 0.0 copy-done.1
  8.1 0.6 reshape.15.gain_s
  8.7 0.0 copy-done.2
  8.7 0.6 reshape.16.gain_t
  9.3 0.0 copy-done.3
  9.3 0.6 reshape.17.gain_m
  9.9 120.5 %shard_map.100 = bf16[4,256,768]{2,1,0:T(8,128)(2,1)} custom-call(bf16[8,256,768]{2,1,0:T(8,128)(2,1)} %clip.1, f32[1,768]{1,0:T(1,128)} %reshape.15.gain_s, f32[1,768]{1,0:T(1,128)} %reshape.16.gain_t, f32[1,768]{1,0:T(1,128)} %reshape.17.gain_m, bf16[768,1152]{1,0:T(8,128)(2,1)} %copy.15.w0, bf16[384,768]{1,0:T(8,128)(2,1)} %w1.1, ...), custom_call_target="tpu_custom_call" | custom-call | flops 22000001024 | bytes 13000000 | tf_op jit(solution)/shard_map/pallas_call | solution.py:328
  130.4 2.7 %copy.18 = bf16[4,256,768]{2,1,0:T(8,128)(2,1)} copy(bf16[4,256,768]{2,1,0:T(8,128)(2,1)} %shard_map.100) | data formatting | bytes 3145728
Async XLA Ops:
  2.6 2.3 %copy-start = (bf16[768,3,384]{2,0,1:T(8,128)(2,1)S(1)}, bf16[768,3,384]{2,0,1:T(8,128)(2,1)}, u32[]{:S(2)}) copy-start(bf16[768,3,384]{2,0,1:T(8,128)(2,1)} %param.16) | copy-start | bytes 5308420
  5.8 2.3 %copy-start.1 = (f32[768]{0:T(1024)S(1)}, f32[768]{0:T(1024)}, u32[]{:S(2)}) copy-start(f32[768]{0:T(1024)} %param.11) | copy-start | bytes 9220
  5.9 2.9 %copy-start.2 = (f32[768]{0:T(1024)S(1)}, f32[768]{0:T(1024)}, u32[]{:S(2)}) copy-start(f32[768]{0:T(1024)} %param.12) | copy-start | bytes 9220
  5.9 3.4 %copy-start.3 = (f32[768]{0:T(1024)S(1)}, f32[768]{0:T(1024)}, u32[]{:S(2)}) copy-start(f32[768]{0:T(1024)} %param.13) | copy-start | bytes 9220

commit v3 on v2

--- a/solution.py
+++ b/solution.py
@@ -80,13 +80,17 @@
     x, normed, qkv_s, qkv_t, mixed, positions,
     send1, recv1, send2, recv2, perm,
     f0, f1, f2, f3, f4, f5,
-    x_sem, own_sem, z_send, z_recv, core_send, core_recv, round_sem,
+    x_sem, own_sem, z_send, z_recv, ring_send, ring_recv, far_recv, core_send, core_recv, round_sem,
     a_send, a_recv, b_send, b_recv,
 ):
     s, m = lax.axis_index("seq"), lax.axis_index("mp")
     me = s * 2 + m
     group, place = me // GROUP, lax.rem(me, GROUP)
     z_hi, core = s // 32, lax.rem(s, 2)
+    x_at, y_at = lax.rem(s // 8, 4), lax.rem(s // 2, 4)
+    ring_place = x_at * (1 - core) + y_at * core
+    above = (lax.rem(z_hi + m, 2) * 32 + lax.rem(s, 32), 1 - m)
+    below = (lax.rem(z_hi + 1 - m, 2) * 32 + lax.rem(s, 32), 1 - m)
     owned = (w0, w1, w2, w3, w4, w5)
     full = (f0, f1, f2, f3, f4, f5)
 
@@ -101,42 +105,63 @@
     def device(index):
         return (index // 2, lax.rem(index, 2))
 
+    def copy(ref, send_sem, recv_sem, to):
+        pltpu.make_async_remote_copy(
+            src_ref=ref, dst_ref=ref, send_sem=send_sem, recv_sem=recv_sem, device_id=to, device_id_type=MESH
+        ).start()
+
+    def landed(ref, sem):
+        pltpu.make_async_copy(ref, ref, sem).wait()
+
     def load(k):
-        return pltpu.make_async_copy(owned[k], part(k, m, 0, ROWS[k]), own_sem.at[k])
-
-    def z_start(k):
-        rows = ROWS[k] // 4
-        start = (z_hi * 2 + core) * rows
-        for other in range(2):
-            pltpu.make_async_remote_copy(
-                src_ref=owned[k].at[pl.ds(pl.multiple_of(start, 16), rows)],
-                dst_ref=part(k, m, start, rows),
-                send_sem=z_send.at[k],
-                recv_sem=z_recv.at[k, z_hi],
-                device_id=(other * 32 + lax.rem(s, 32), 1 - m),
-                device_id_type=MESH,
-            ).start()
-
-    def z_forward(k):
-        rows = ROWS[k] // 4
-        for source in range(2):
-            piece = part(k, 1 - m, (source * 2 + core) * rows, rows)
-            pltpu.make_async_copy(piece, piece, z_recv.at[k, source]).wait()
-            pltpu.make_async_remote_copy(
-                src_ref=piece,
-                dst_ref=piece,
-                send_sem=core_send.at[k],
-                recv_sem=core_recv.at[k],
-                device_id=device(flip(2)),
-                device_id_type=MESH,
-            ).start()
-
-    def half_bytes(k, sem):
-        block = part(k, 0, 0, ROWS[k] // 2)
-        pltpu.make_async_copy(block, block, sem.at[k]).wait()
-
-    def z_finish(k):
-        half_bytes(k, core_recv)
+        if k in (0, 2):
+            for c in range(3):
+                columns = full[k].at[m, :, c * HALF : (c + 1) * HALF]
+                pltpu.make_async_copy(owned[k].at[c], columns, own_sem.at[k]).start()
+        else:
+            pltpu.make_async_copy(owned[k], part(k, m, 0, ROWS[k]), own_sem.at[k]).start()
+
+    def loaded(k):
+        landed(part(k, m, 0, ROWS[k]), own_sem.at[k])
+
+    def quarter(k, half, step, sub=None):
+        rows = ROWS[k] // 8
+        start = core * (ROWS[k] // 2) + lax.rem(ring_place + step + 4, 4) * rows
+        if sub is None:
+            return part(k, half, start, rows)
+        if STACKED[k]:
+            return part(k, half, start, rows).at[:, sub * HALF : (sub + 1) * HALF]
+        return part(k, half, start + sub * (rows // 2), rows // 2)
+
+    def ring(step):
+        to_x, to_y = lax.rem(x_at + step * (1 - core) + 4, 4), lax.rem(y_at + step * core + 4, 4)
+        return (z_hi * 32 + to_x * 8 + to_y * 2 + core, m)
+
+    def fetch_z(k):
+        loaded(k)
+        for sub in range(2):
+            copy(quarter(k, m, 0, sub), z_send.at[k], z_recv.at[k, sub], above if sub == 0 else below)
+
+    def fetch_ring(k):
+        for sub in range(2):
+            landed(quarter(k, 1 - m, 0, sub), z_recv.at[k, sub])
+        for way, step in enumerate((1, -1)):
+            copy(quarter(k, 1 - m, 0), ring_send.at[k], ring_recv.at[k, way], ring(step))
+        copy(quarter(k, 1 - m, 0), core_send.at[k], core_recv.at[k], device(flip(2)))
+
+    def fetch_far(k):
+        for way, step in enumerate((1, -1)):
+            landed(quarter(k, 1 - m, -step), ring_recv.at[k, way])
+            copy(quarter(k, 1 - m, -step, way), ring_send.at[k], far_recv.at[k, way], ring(step))
+            copy(quarter(k, 1 - m, -step), core_send.at[k], core_recv.at[k], device(flip(2)))
+
+    def fetch_last(k):
+        for way in range(2):
+            landed(quarter(k, 1 - m, 2, way), far_recv.at[k, way])
+        copy(quarter(k, 1 - m, 2), core_send.at[k], core_recv.at[k], device(flip(2)))
+
+    def fetched(k):
+        landed(part(k, 0, 0, ROWS[k] // 2), core_recv.at[k])
 
     def exchange(b, to, send, recv, send_sem, recv_sem):
         @pl.when(b == 0)
@@ -164,15 +189,16 @@
         return block[...]
 
     barrier = pltpu.get_barrier_semaphore()
-    for bit in (1, 2, 4, 8, 16, 32, 64):
-        pl.semaphore_signal(barrier, inc=1, device_id=device(flip(bit)), device_id_type=MESH)
-    pl.semaphore_signal(
-        barrier, inc=1, device_id=(lax.rem(s + 32, 64), 1 - m), device_id_type=MESH
-    )
+    greeted = [device(flip(bit)) for bit in (2, 8, 32, 64)] + [above, below]
+    for step in (1, 3):
+        greeted.append((z_hi * 32 + lax.rem(x_at + step, 4) * 8 + y_at * 2 + core, m))
+        greeted.append((z_hi * 32 + x_at * 8 + lax.rem(y_at + step, 4) * 2 + core, m))
+    for other in greeted:
+        pl.semaphore_signal(barrier, inc=1, device_id=other, device_id_type=MESH)
     own_frames = pltpu.make_async_copy(clip.at[pl.ds(m * 4, 4)], x, x_sem)
     own_frames.start()
     for k in range(6):
-        load(k).start()
+        load(k)
     perm[0] = one_hot((4, 5, 1), (3, 1, 8), (2, 1, 0), (0, 2, 6))
     perm[1] = one_hot((8, 1, 3), (7, 1, 2), (2, 5, 4), (0, 2, 0))
     perm[2] = one_hot((4, 5, 2), (3, 1, 8), (2, 1, 7), (0, 2, 0))
@@ -181,23 +207,27 @@
 
     @pl.loop(0, 4)
     def _(f):
-        normed[pl.ds(pl.multiple_of(f * TOKENS, TOKENS), TOKENS)] = layer_norm(x[f], gain_s[...])
-
-    pl.semaphore_wait(barrier, 8)
-    z_start(0)
-    z_start(1)
+        normed[pl.ds(pl.multiple_of(f * TOKENS, TOKENS), TOKENS)] = layer_norm(x[f], gain_s[...].reshape(1, D))
+
+    pl.semaphore_wait(barrier, len(greeted))
+    fetch_z(0)
+    fetch_z(1)
 
     columns = lax.broadcasted_iota(jnp.int32, (1, 3 * HALF), 1)
     scale = jnp.where(columns < HALF, Q_SCALE, 1.0).astype(F32)
 
-    def spatial_heads(half):
+    def spatial_heads(half, after_qkv, beside):
         @pl.loop(0, 4)
         def _(f):
             rows = pl.ds(pl.multiple_of(f * TOKENS, TOKENS), TOKENS)
             qkv_s[rows] = (dot(normed[rows], f0[half]) * scale).astype(BF16)
 
+        after_qkv()
+
         @pl.loop(0, 4)
         def _(f):
+            for turn, service in beside.items():
+                pl.when(f == turn)(service)
             rows = pl.ds(pl.multiple_of(f * TOKENS, TOKENS), TOKENS)
             for pair in range(3):
                 c = pair * 128
@@ -207,21 +237,47 @@
                     qkv_s[rows, 2 * HALF + c : 2 * HALF + c + 128],
                 )
 
-    load(0).wait()
-    spatial_heads(m)
-    for r in range(7):
-        pl.semaphore_signal(
-            round_sem.at[r], inc=1, device_id=device(flip(1 << r)), device_id_type=MESH
-        )
-        pl.semaphore_wait(round_sem.at[r], 1)
-    z_forward(0)
-    z_forward(1)
-    z_start(2)
-    z_start(3)
-    z_finish(0)
-    spatial_heads(1 - m)
-    load(1).wait()
-    z_finish(1)
+    def rounds(low, high):
+        for r in range(low, high):
+            pl.semaphore_signal(
+                round_sem.at[r], inc=1, device_id=device(flip((16, 32, 4, 8, 2, 1, 64)[r])), device_id_type=MESH
+            )
+            pl.semaphore_wait(round_sem.at[r], 1)
+
+    def service_a():
+        fetch_ring(0)
+        fetch_ring(1)
+        fetch_z(2)
+        fetch_z(3)
+        rounds(0, 2)
+
+    def service_b():
+        fetch_far(0)
+        fetch_far(1)
+        fetch_z(4)
+        fetch_z(5)
+        rounds(2, 4)
+
+    def service_c():
+        fetch_ring(2)
+        fetch_ring(3)
+        rounds(4, 7)
+
+    def service_d():
+        fetch_ring(4)
+        fetch_ring(5)
+
+    def service_e():
+        fetch_far(2)
+        fetch_far(3)
+
+    spatial_heads(m, service_a, {2: service_b})
+    fetch_last(0)
+    fetch_last(1)
+    service_c()
+    fetched(0)
+    spatial_heads(1 - m, service_d, {2: service_e})
+    fetched(1)
 
     @pl.loop(0, 4)
     def _(f):
@@ -238,19 +294,18 @@
         send1[pl.ds(pl.multiple_of(to * 512, 512), 512)] = dot(perm[0], block).astype(BF16)
         exchange(b, to, send1, recv1, a_send, a_recv)
 
-    z_start(4)
-    z_start(5)
-    z_forward(2)
-    z_forward(3)
-    load(2).wait()
-    z_finish(2)
+    fetch_last(2)
+    fetch_last(3)
+    fetch_far(4)
+    fetch_far(5)
+    fetched(2)
 
     @pl.loop(0, 4)
     def _(b):
         source = lax.rem(group + 4 - b, 4)
         block = dot(perm[1], arrived(recv1, a_recv, source)).astype(BF16)
         tokens = jnp.concatenate([block[:TOKENS], block[TOKENS:]], axis=1)
-        normal = layer_norm(tokens, gain_t[...])
+        normal = layer_norm(tokens, gain_t[...].reshape(1, D))
         for p in range(2):
             rows = pl.ds(pl.multiple_of(p * 512 + b * 128, 128), 128)
             positions[rows] = tokens[p * 128 : (p + 1) * 128]
@@ -276,14 +331,11 @@
                     qkv_t[half, every, 2 * HALF + c : 2 * HALF + c + 128],
                 )
 
-        z_forward(4 + p)
-
-    load(3).wait()
-    z_finish(3)
-    load(4).wait()
-    z_finish(4)
-    load(5).wait()
-    z_finish(5)
+        fetch_last(4 + p)
+
+    fetched(3)
+    fetched(4)
+    fetched(5)
 
     @pl.loop(0, 4)
     def _(b):
@@ -291,7 +343,7 @@
         total = dot(jnp.concatenate([mixed[r] for r in rows], axis=0), f3[...])
         tokens = jnp.concatenate([positions[r] for r in rows], axis=0)
         tokens = (tokens.astype(F32) + total).astype(BF16)
-        normal = layer_norm(tokens, gain_m[...])
+        normal = layer_norm(tokens, gain_m[...].reshape(1, D))
         total = tokens.astype(F32)
         for j in range(4):
             up = dot(normal, f4[j // 2, :, (j % 2) * D : (j % 2 + 1) * D])
@@ -316,13 +368,13 @@
         sent = send.at[pl.ds(0, (DEVICES - 1) * 16)]
         pltpu.make_async_copy(sent, sent, sem).wait()
     for k in range(6):
-        half_bytes(k, z_send)
-        half_bytes(k, core_send)
+        landed(part(k, 0, 0, ROWS[k] // 8), z_send.at[k])
+        landed(part(k, 0, 0, ROWS[k] // 8 * 3), ring_send.at[k])
+        landed(part(k, 0, 0, ROWS[k] // 2), core_send.at[k])
 
 
 def per_device(clip, gain_s, gain_t, gain_m, w0, w1, w2, w3, w4, w5):
-    w0, w2 = w0.reshape(D, 3 * HALF), w2.reshape(D, 3 * HALF)
-    gains = [g.reshape(1, D) for g in (gain_s, gain_t, gain_m)]
+    w0, w2 = jnp.swapaxes(w0, 0, 1), jnp.swapaxes(w2, 0, 1)
     vmem, anywhere = pl.BlockSpec(memory_space=pltpu.VMEM), pl.BlockSpec(memory_space=pl.ANY)
     dma = pltpu.SemaphoreType.DMA
     return pl.pallas_call(
@@ -353,6 +405,9 @@
             dma((6,)),
             dma((6, 2)),
             dma((6,)),
+            dma((6, 2)),
+            dma((6, 2)),
+            dma((6,)),
             dma((6,)),
             pltpu.SemaphoreType.REGULAR((7,)),
             dma,
@@ -366,7 +421,7 @@
         cost_estimate=pl.CostEstimate(
             flops=22 * 10**9, bytes_accessed=13 * 10**6, transcendentals=12 * 10**6
         ),
-    )(clip, *gains, w0, w1, w2, w3, w4, w5)
+    )(clip, gain_s, gain_t, gain_m, w0, w1, w2, w3, w4, w5)
 
 
 def solution(mesh):

time: 133 us -> 112 us (0.84)
  Pallas kernels: 120 us -> 109 us
  local copies, waits for them, and re-layouts: 12.5 us -> 2.65 us
    pallas_call x1, Pallas kernels: 120 us -> 109 us  [per_device(): pl.pallas_call(kernel, out_shape=jax.ShapeDtypeStruct((4, 256, D), BF16),...]
    reshape x5 -> x0, local copies, waits for them, and re-layouts: 6.25 us -> none  [the longest x2 4.5 us: per_device(): w0, w2 = (w0.reshape(D, 3 * HALF), w2.reshape(D, 3 * HALF))]
    unnamed x11 -> x1, local copies, waits for them, and re-layouts: 6.24 us -> 2.65 us
where the time goes in v3:
time: 112 us
  Pallas kernels  109 us (97%)
  local copies, waits for them, and re-layouts  2.65 us (2%)
    pallas_call x1, Pallas kernels, per_device(): pl.pallas_call(kernel, out_shape=jax.ShapeDtypeStruct((4, 256, D), BF16),...  109 us
    unnamed x1, local copies, waits for them, and re-layouts  2.65 us

profile of v3, /device:TPU:1, one launch (start us, length us, event | category | flops | bytes accessed | tf_op | source)
XLA Modules:
  0.0 112.0 jit_solution(1320843552755219280)
XLA Ops:
  0.0 109.3 %shard_map.100 = bf16[4,256,768]{2,1,0:T(8,128)(2,1)} custom-call(bf16[8,256,768]{2,1,0:T(8,128)(2,1)} %clip.1, f32[768]{0:T(1024)} %gain_s.1, f32[768]{0:T(1024)} %gain_t.1, f32[768]{0:T(1024)} %gain_m.1, bf16[3,768,384]{2,1,0:T(8,128)(2,1)} %bitcast.2, bf16[384,768]{1,0:T(8,128)(2,1)} %w1.1, bf16[3,768,384]{2,1,0:T(8,128)(2,1)} %bitcast.3, ...), custom_call_target="tpu_custom_call" | custom-call | flops 22000001024 | bytes 13000000 | tf_op jit(solution)/shard_map/pallas_call | solution.py:380
  109.3 2.7 %copy.12 = bf16[4,256,768]{2,1,0:T(8,128)(2,1)} copy(bf16[4,256,768]{2,1,0:T(8,128)(2,1)} %shard_map.100) | data formatting | bytes 3145728

commit v4 on v3

v4 whole, which is shorter than its diff:
```python
import functools
import math

import jax
import jax.numpy as jnp
from jax import lax
from jax.experimental import pallas as pl
from jax.experimental.pallas import tpu as pltpu
from jax.sharding import PartitionSpec as P

MESH = pl.DeviceIdType.MESH
F32, BF16 = jnp.float32, jnp.bfloat16
HEAD_DIM = 64
D = 768
HALF = 384
TOKENS = 256
CHIPS = 64
PACKED = 16 * 24
GROUP = 16
Q_SCALE = math.log2(math.e) * HEAD_DIM**-0.5
ROWS = (768, 384, 768, 384, 768, 1536)
STACKED = (False, True, False, True, False, True)


def dot(a, b):
    return jnp.dot(a, b, preferred_element_type=F32)


def layer_norm(values, gain):
    values = values.astype(F32)
    center = values - jnp.mean(values, axis=-1, keepdims=True)
    spread = jnp.mean(center * center, axis=-1, keepdims=True)
    return (center * lax.rsqrt(spread + 1e-05) * gain).astype(BF16)


def attend_pair(query, keys, vals):
    first = lax.broadcasted_iota(jnp.int32, (1, 128), 1) < HEAD_DIM
    zero = jnp.zeros_like(query)
    one = jnp.ones_like(vals)
    outs = []
    for mine in (first, jnp.logical_not(first)):
        scores = lax.dot_general(
            jnp.where(mine, query, zero), keys, (((1,), (1,)), ((), ())), preferred_element_type=F32
        )
        weights = jnp.exp2(scores).astype(BF16)
        filled = jnp.where(mine, vals, one)
        both = jnp.concatenate([filled * BF16(2.0**-8), filled * BF16(2.0**24)], axis=1)
        outs.append(dot(weights, both))
    out_a, out_b = outs
    low_top, low_sum = jnp.where(first, out_a[:, :128], out_b[:, :128]), jnp.where(
        first, out_b[:, :128], out_a[:, :128]
    )
    high_top, high_sum = jnp.where(first, out_a[:, 128:], out_b[:, 128:]), jnp.where(
        first, out_b[:, 128:], out_a[:, 128:]
    )
    low_sum = pltpu.roll(low_sum, HEAD_DIM, 1)
    high_sum = pltpu.roll(high_sum, HEAD_DIM, 1)
    large = low_sum > 2.0**-8
    return (jnp.where(large, low_top, high_top) / jnp.where(large, low_sum, high_sum)).astype(BF16)


def gelu(value):
    return 0.5 * value * (1.0 + lax.erf(value * 0.5**0.5))


def one_hot(rows_packed):
    packed = lax.broadcasted_iota(jnp.int32, (PACKED, PACKED), 0 if rows_packed else 1)
    plain = lax.broadcasted_iota(jnp.int32, (PACKED, PACKED), 1 if rows_packed else 0)
    device = (packed * 2731) >> 16
    rest = packed - device * 24
    return jnp.where(plain == ((rest >> 2) << 6) + ((rest & 3) << 4) + device, 1.0, 0.0).astype(BF16)


def pack(tokens, perm):
    sides = [
        jnp.concatenate([tokens[u * 64 : (u + 1) * 64, c * 128 : (c + 1) * 128] for c in range(6)], axis=0)
        for u in range(2)
    ]
    made = dot(perm, jnp.concatenate(sides, axis=1))
    return [made[:, u * 128 : (u + 1) * 128].reshape(16, 24, 128).astype(BF16) for u in range(2)]


def unpack(blocks, perm):
    sides = [blocks[u].astype(F32).reshape(PACKED, 128).astype(BF16) for u in range(2)]
    made = dot(perm, jnp.concatenate(sides, axis=1)).astype(BF16)
    return jnp.concatenate(
        [
            jnp.concatenate([made[c * 64 : (c + 1) * 64, u * 128 : (u + 1) * 128] for c in range(6)], axis=1)
            for u in range(2)
        ],
        axis=0,
    )


def kernel(
    clip, gain_s, gain_t, gain_m, w0, w1, w2, w3, w4, w5, out,
    x, normed, qkv_s, qkv_t, mixed, positions,
    send1, recv1, send2, recv2, cross1, cross2, perm,
    f0, f1, f2, f3, f4, f5,
    x_sem, own_sem, z_send, z_recv, ring_send, ring_recv, far_recv, core_send, core_recv, round_sem,
    a_send, a_recv, b_send, b_recv, c_send, c_recv, d_send, d_recv,
):
    s, m = lax.axis_index("seq"), lax.axis_index("mp")
    me = s * 2 + m
    z_hi, core = s // 32, lax.rem(s, 2)
    x_at, y_at = lax.rem(s // 8, 4), lax.rem(s // 2, 4)
    chip = lax.rem(x_at + y_at + z_hi * 2 + m, 4) * GROUP + x_at * 4 + y_at
    group, place = chip // GROUP, lax.rem(chip, GROUP)
    ring_place = x_at * (1 - core) + y_at * core
    above = (lax.rem(z_hi + m, 2) * 32 + lax.rem(s, 32), 1 - m)
    below = (lax.rem(z_hi + 1 - m, 2) * 32 + lax.rem(s, 32), 1 - m)
    owned = (w0, w1, w2, w3, w4, w5)
    full = (f0, f1, f2, f3, f4, f5)

    def part(k, half, start, rows):
        if STACKED[k]:
            return full[k].at[pl.ds(pl.multiple_of(half * ROWS[k] + start, 16), rows)]
        return full[k].at[half, pl.ds(pl.multiple_of(start, 16), rows)]

    def flip(bit):
        return me + bit * (1 - 2 * lax.rem(me // bit, 2))

    def device(index):
        return (index // 2, lax.rem(index, 2))

    def copy(ref, send_sem, recv_sem, to):
        pltpu.make_async_remote_copy(
            src_ref=ref, dst_ref=ref, send_sem=send_sem, recv_sem=recv_sem, device_id=to, device_id_type=MESH
        ).start()

    def landed(ref, sem):
        pltpu.make_async_copy(ref, ref, sem).wait()

    def load(k):
        if k in (0, 2):
            for c in range(3):
                columns = full[k].at[m, :, c * HALF : (c + 1) * HALF]
                pltpu.make_async_copy(owned[k].at[c], columns, own_sem.at[k]).start()
        else:
            pltpu.make_async_copy(owned[k], part(k, m, 0, ROWS[k]), own_sem.at[k]).start()

    def loaded(k):
        landed(part(k, m, 0, ROWS[k]), own_sem.at[k])

    def quarter(k, half, step, sub=None):
        rows = ROWS[k] // 8
        start = core * (ROWS[k] // 2) + lax.rem(ring_place + step + 4, 4) * rows
        if sub is None:
            return part(k, half, start, rows)
        if STACKED[k]:
            return part(k, half, start, rows).at[:, sub * HALF : (sub + 1) * HALF]
        return part(k, half, start + sub * (rows // 2), rows // 2)

    def ring(step):
        to_x, to_y = lax.rem(x_at + step * (1 - core) + 4, 4), lax.rem(y_at + step * core + 4, 4)
        return (z_hi * 32 + to_x * 8 + to_y * 2 + core, m)

    def fetch_z(k):
        loaded(k)
        for sub in range(2):
            copy(quarter(k, m, 0, sub), z_send.at[k], z_recv.at[k, sub], above if sub == 0 else below)

    def fetch_ring(k):
        for sub in range(2):
            landed(quarter(k, 1 - m, 0, sub), z_recv.at[k, sub])
        for way, step in enumerate((1, -1)):
            copy(quarter(k, 1 - m, 0), ring_send.at[k], ring_recv.at[k, way], ring(step))
        copy(quarter(k, 1 - m, 0), core_send.at[k], core_recv.at[k], device(flip(2)))

    def fetch_far(k):
        for way, step in enumerate((1, -1)):
            landed(quarter(k, 1 - m, -step), ring_recv.at[k, way])
            copy(quarter(k, 1 - m, -step, way), ring_send.at[k], far_recv.at[k, way], ring(step))
            copy(quarter(k, 1 - m, -step), core_send.at[k], core_recv.at[k], device(flip(2)))

    def fetch_last(k):
        for way in range(2):
            landed(quarter(k, 1 - m, 2, way), far_recv.at[k, way])
        copy(quarter(k, 1 - m, 2), core_send.at[k], core_recv.at[k], device(flip(2)))

    def fetched(k):
        landed(part(k, 0, 0, ROWS[k] // 2), core_recv.at[k])

    def exchange(p, b, to, send, recv, send_sem, recv_sem):
        def step(i):
            column = lax.rem(i + place, GROUP)
            dest = to * GROUP + column
            x_to, y_to = column // 4, lax.rem(column, 4)
            z_to = lax.rem(to + 8 - x_to - y_to, 4)
            pltpu.make_async_remote_copy(
                src_ref=send.at[p, dest],
                dst_ref=recv.at[p, chip],
                send_sem=send_sem.at[p],
                recv_sem=recv_sem.at[p, group],
                device_id=((z_to // 2) * 32 + x_to * 8 + y_to * 2 + core, lax.rem(z_to, 2)),
                device_id_type=MESH,
            ).start()

        @pl.when(b == 0)
        def _():
            pltpu.make_async_copy(send.at[p, chip], recv.at[p, chip], recv_sem.at[p, group]).start()

        @pl.when(b != 0)
        def _():
            step(0)

        for i in range(1, GROUP):
            step(i)

    def put(p, b, to, tokens, order, send, recv, send_sem, recv_sem):
        for block, to_core in zip(pack(tokens, perm[0]), order):
            send[p, pl.ds(to * GROUP, GROUP), to_core] = block
        exchange(p, b, to, send, recv, send_sem, recv_sem)

    def hand_on(p, source, recv, recv_sem, crossed, cross_send, cross_recv):
        chips = pl.ds(source * GROUP, GROUP)
        landed(recv.at[p, chips], recv_sem.at[p, source])
        pltpu.make_async_remote_copy(
            src_ref=recv.at[p, chips, 1 - core],
            dst_ref=crossed.at[p, chips],
            send_sem=cross_send.at[p],
            recv_sem=cross_recv.at[p, source],
            device_id=device(flip(2)),
            device_id_type=MESH,
        ).start()

    def take(p, source, recv, crossed, cross_recv):
        chips = pl.ds(source * GROUP, GROUP)
        landed(crossed.at[p, chips], cross_recv.at[p, source])
        return unpack((recv[p, chips, core], crossed[p, chips]), perm[1])

    barrier = pltpu.get_barrier_semaphore()
    greeted = [device(flip(bit)) for bit in (2, 8, 32, 64)] + [above, below]
    for step in (1, 3):
        greeted.append((z_hi * 32 + lax.rem(x_at + step, 4) * 8 + y_at * 2 + core, m))
        greeted.append((z_hi * 32 + x_at * 8 + lax.rem(y_at + step, 4) * 2 + core, m))
    for other in greeted:
        pl.semaphore_signal(barrier, inc=1, device_id=other, device_id_type=MESH)
    own_frames = pltpu.make_async_copy(clip.at[pl.ds(m * 4, 4)], x, x_sem)
    own_frames.start()
    for k in range(6):
        load(k)
    pl.semaphore_wait(barrier, len(greeted))
    fetch_z(0)
    fetch_z(1)
    perm[0] = one_hot(True)
    perm[1] = one_hot(False)
    own_frames.wait()

    @pl.loop(0, 4)
    def _(f):
        normed[pl.ds(pl.multiple_of(f * TOKENS, TOKENS), TOKENS)] = layer_norm(x[f], gain_s[...].reshape(1, D))

    columns = lax.broadcasted_iota(jnp.int32, (1, 3 * HALF), 1)
    scale = jnp.where(columns < HALF, Q_SCALE, 1.0).astype(F32)

    def spatial_qkv(half):
        @pl.loop(0, 4)
        def _(f):
            rows = pl.ds(pl.multiple_of(f * TOKENS, TOKENS), TOKENS)
            qkv_s[rows] = (dot(normed[rows], f0[half]) * scale).astype(BF16)

    def spatial_heads(half, f, start, count):
        rows = pl.ds(pl.multiple_of(f * TOKENS + start, count), count)
        every = pl.ds(pl.multiple_of(f * TOKENS, TOKENS), TOKENS)
        for pair in range(3):
            c = pair * 128
            mixed[rows, pl.ds(pl.multiple_of(half * HALF + c, 128), 128)] = attend_pair(
                qkv_s[rows, c : c + 128],
                qkv_s[every, HALF + c : HALF + c + 128],
                qkv_s[every, 2 * HALF + c : 2 * HALF + c + 128],
            )

    def rounds(low, high):
        for r in range(low, high):
            pl.semaphore_signal(
                round_sem.at[r], inc=1, device_id=device(flip((16, 32, 4, 8, 2, 1, 64)[r])), device_id_type=MESH
            )
            pl.semaphore_wait(round_sem.at[r], 1)

    spatial_qkv(m)
    fetch_ring(0)
    fetch_ring(1)
    fetch_z(2)
    fetch_z(3)
    rounds(0, 2)

    @pl.loop(0, 4)
    def _(f):
        @pl.when(f == 2)
        def _():
            fetch_far(0)
            fetch_far(1)
            fetch_z(4)
            fetch_z(5)
            rounds(2, 4)

        spatial_heads(m, f, 0, TOKENS)

    fetch_last(0)
    fetch_last(1)
    fetch_ring(2)
    fetch_ring(3)
    rounds(4, 7)
    fetched(0)
    spatial_qkv(1 - m)

    @pl.loop(0, 2)
    def _(p):
        @pl.when(p == 1)
        def _():
            fetch_last(2)
            fetch_last(3)
            fetch_ring(4)
            fetch_ring(5)

        @pl.loop(0, 4)
        def _(f):
            @pl.when(jnp.logical_and(p == 0, f == 2))
            def _():
                fetch_far(2)
                fetch_far(3)

            spatial_heads(1 - m, f, p * 128, 128)

        @pl.when(p == 0)
        def _():
            fetched(1)

        patches = pl.ds(pl.multiple_of(p * 128, 128), 128)

        @pl.loop(0, 2)
        def _(pair):
            rows = [pl.ds(pl.multiple_of((pair * 2 + i) * TOKENS + p * 128, 128), 128) for i in range(2)]
            total = dot(jnp.concatenate([mixed[r] for r in rows], axis=0), f1[...])
            for i in range(2):
                f = pair * 2 + i
                x[f, patches] = (x[f, patches].astype(F32) + total[i * 128 : (i + 1) * 128]).astype(BF16)

        @pl.loop(0, 4)
        def _(b):
            to = lax.rem(group + b, 4)
            tokens = [
                x[f, pl.ds(pl.multiple_of(p * 128 + u * CHIPS + to * GROUP, GROUP), GROUP)]
                for u in range(2)
                for f in range(4)
            ]
            put(p, b, to, jnp.concatenate(tokens, axis=0), (0, 1), send1, recv1, a_send, a_recv)

    fetched(2)

    def hand_on_a(p):
        @pl.loop(0, 4)
        def _(b):
            hand_on(p, lax.rem(group + 4 - b, 4), recv1, a_recv, cross1, c_send, c_recv)

    def hand_on_b(p):
        @pl.loop(0, 4)
        def _(b):
            hand_on(p, lax.rem(group + b, 4), recv2, b_recv, cross2, d_send, d_recv)

    hand_on_a(0)

    @pl.loop(0, 2)
    def _(p):
        @pl.loop(0, 2)
        def _(pair):
            rows = pl.ds(pl.multiple_of(p * 512 + pair * TOKENS, TOKENS), TOKENS)
            tokens = jnp.concatenate(
                [take(p, lax.rem(group + 4 - pair * 2 - i, 4), recv1, cross1, c_recv) for i in range(2)], axis=0
            )
            positions[rows] = tokens
            normal = layer_norm(tokens, gain_t[...].reshape(1, D))
            for half in range(2):
                qkv_t[half, rows] = (dot(normal, f2[half]) * scale).astype(BF16)

        @pl.when(p == 0)
        def _():
            fetch_far(4)
            fetch_far(5)

        @pl.loop(0, 4)
        def _(t):
            @pl.when(jnp.logical_and(p == 0, t == 2))
            def _():
                fetch_last(4)
                fetch_last(5)

            half = t // 2
            every = pl.ds(pl.multiple_of(p * 512, 512), 512)
            rows = pl.ds(pl.multiple_of(p * 512 + lax.rem(t, 2) * TOKENS, TOKENS), TOKENS)
            for pair in range(3):
                c = pair * 128
                mixed[rows, pl.ds(pl.multiple_of(half * HALF + c, 128), 128)] = attend_pair(
                    qkv_t[half, rows, c : c + 128],
                    qkv_t[half, every, HALF + c : HALF + c + 128],
                    qkv_t[half, every, 2 * HALF + c : 2 * HALF + c + 128],
                )

        @pl.when(p == 0)
        def _():
            fetched(3)
            fetched(4)
            fetched(5)
            hand_on_a(1)

        @pl.when(p == 1)
        def _():
            hand_on_b(0)

        @pl.loop(0, 2)
        def _(pair):
            rows = pl.ds(pl.multiple_of(p * 512 + pair * TOKENS, TOKENS), TOKENS)
            tokens = (positions[rows].astype(F32) + dot(mixed[rows], f3[...])).astype(BF16)
            normal = layer_norm(tokens, gain_m[...].reshape(1, D))
            total = tokens.astype(F32)
            for j in range(4):
                up = dot(normal, f4[j // 2, :, (j % 2) * D : (j % 2 + 1) * D])
                total = total + dot(gelu(up).astype(BF16), f5[j * D : (j + 1) * D])
            done = total.astype(BF16)
            for i in range(2):
                b = pair * 2 + i
                to = lax.rem(group + 4 - b, 4)
                put(p, b, to, done[i * 128 : (i + 1) * 128], (core, 1 - core), send2, recv2, b_send, b_recv)

    hand_on_b(1)

    @pl.loop(0, 2)
    def _(p):
        @pl.loop(0, 4)
        def _(b):
            source = lax.rem(group + b, 4)
            tokens = take(p, source, recv2, cross2, d_recv)
            for u, of_core in enumerate((core, 1 - core)):
                rows = pl.ds(pl.multiple_of(p * 128 + of_core * CHIPS + source * GROUP, GROUP), GROUP)
                for f in range(4):
                    out[f, rows] = tokens[u * 64 + f * 16 : u * 64 + (f + 1) * 16]

    for p in range(2):
        for send, sem in ((send1, a_send), (send2, b_send)):
            landed(send.at[p, pl.ds(0, CHIPS - 1)], sem.at[p])
        for crossed, sem in ((cross1, c_send), (cross2, d_send)):
            landed(crossed.at[p], sem.at[p])
    for k in range(6):
        landed(part(k, 0, 0, ROWS[k] // 8), z_send.at[k])
        landed(part(k, 0, 0, ROWS[k] // 8 * 3), ring_send.at[k])
        landed(part(k, 0, 0, ROWS[k] // 2), core_send.at[k])


def per_device(clip, gain_s, gain_t, gain_m, w0, w1, w2, w3, w4, w5):
    w0, w2 = jnp.swapaxes(w0, 0, 1), jnp.swapaxes(w2, 0, 1)
    vmem, anywhere = pl.BlockSpec(memory_space=pltpu.VMEM), pl.BlockSpec(memory_space=pl.ANY)
    dma = pltpu.SemaphoreType.DMA
    return pl.pallas_call(
        kernel,
        out_shape=jax.ShapeDtypeStruct((4, 256, D), BF16),
        in_specs=[anywhere, vmem, vmem, vmem] + [anywhere] * 6,
        out_specs=vmem,
        scratch_shapes=[
            pltpu.VMEM((4, 256, D), BF16),
            pltpu.VMEM((1024, D), BF16),
            pltpu.VMEM((1024, 3 * HALF), BF16),
            pltpu.VMEM((2, 1024, 3 * HALF), BF16),
            pltpu.VMEM((1024, D), BF16),
            pltpu.VMEM((1024, D), BF16),
            pltpu.VMEM((2, CHIPS, 2, 24, 128), BF16),
            pltpu.VMEM((2, CHIPS, 2, 24, 128), BF16),
            pltpu.VMEM((2, CHIPS, 2, 24, 128), BF16),
            pltpu.VMEM((2, CHIPS, 2, 24, 128), BF16),
            pltpu.VMEM((2, CHIPS, 24, 128), BF16),
            pltpu.VMEM((2, CHIPS, 24, 128), BF16),
            pltpu.VMEM((2, PACKED, PACKED), BF16),
            pltpu.VMEM((2, D, 3 * HALF), BF16),
            pltpu.VMEM((D, D), BF16),
            pltpu.VMEM((2, D, 3 * HALF), BF16),
            pltpu.VMEM((D, D), BF16),
            pltpu.VMEM((2, D, 1536), BF16),
            pltpu.VMEM((3072, D), BF16),
            dma,
            dma((6,)),
            dma((6,)),
            dma((6, 2)),
            dma((6,)),
            dma((6, 2)),
            dma((6, 2)),
            dma((6,)),
            dma((6,)),
            pltpu.SemaphoreType.REGULAR((7,)),
            dma((2,)),
            dma((2, 4)),
            dma((2,)),
            dma((2, 4)),
            dma((2,)),
            dma((2, 4)),
            dma((2,)),
            dma((2, 4)),
        ],
        compiler_params=pltpu.CompilerParams(
            collective_id=0, has_side_effects=True, vmem_limit_bytes=60 << 20
        ),
        cost_estimate=pl.CostEstimate(
            flops=22 * 10**9, bytes_accessed=13 * 10**6, transcendentals=12 * 10**6
        ),
    )(clip, gain_s, gain_t, gain_m, w0, w1, w2, w3, w4, w5)


def solution(mesh):
    return jax.shard_map(
        per_device,
        mesh=mesh,
        in_specs=(
            P("seq", None, None),
            P(),
            P(),
            P(),
            P(None, None, "mp"),
            P("mp", None),
            P(None, None, "mp"),
            P("mp", None),
            P(None, "mp"),
            P("mp", None),
        ),
        out_specs=P(("seq", "mp"), None, None),
        check_vma=False,
    )
```

time: 112 us -> 106 us (0.946)
  Pallas kernels: 109 us -> 103 us
    pallas_call x1, Pallas kernels: 109 us -> 103 us  [per_device(): pl.pallas_call(kernel, out_shape=jax.ShapeDtypeStruct((4, 256, D), BF16),...]
where the time goes in v4:
time: 106 us
  Pallas kernels  103 us (97%)
  local copies, waits for them, and re-layouts  2.65 us (2%)
    pallas_call x1, Pallas kernels, per_device(): pl.pallas_call(kernel, out_shape=jax.ShapeDtypeStruct((4, 256, D), BF16),...  103 us
    unnamed x1, local copies, waits for them, and re-layouts  2.65 us

profile of v4, /device:TPU:1, one launch (start us, length us, event | category | flops | bytes accessed | tf_op | source)
XLA Modules:
  0.0 105.9 jit_solution(16138258569122903457)
XLA Ops:
  0.0 103.3 %shard_map.100 = bf16[4,256,768]{2,1,0:T(8,128)(2,1)} custom-call(bf16[8,256,768]{2,1,0:T(8,128)(2,1)} %clip.1, f32[768]{0:T(1024)} %gain_s.1, f32[768]{0:T(1024)} %gain_t.1, f32[768]{0:T(1024)} %gain_m.1, bf16[3,768,384]{2,1,0:T(8,128)(2,1)} %bitcast.2, bf16[384,768]{1,0:T(8,128)(2,1)} %w1.1, bf16[3,768,384]{2,1,0:T(8,128)(2,1)} %bitcast.3, ...), custom_call_target="tpu_custom_call" | custom-call | flops 22000001024 | bytes 13000000 | tf_op jit(solution)/shard_map/pallas_call | solution.py:454
  103.3 2.7 %copy.12 = bf16[4,256,768]{2,1,0:T(8,128)(2,1)} copy(bf16[4,256,768]{2,1,0:T(8,128)(2,1)} %shard_map.100) | data formatting | bytes 3145728

commit v5 on v4

--- a/solution.py
+++ b/solution.py
@@ -229,6 +229,14 @@
         landed(crossed.at[p, chips], cross_recv.at[p, source])
         return unpack((recv[p, chips, core], crossed[p, chips]), perm[1])
 
+    def greet(r):
+        if r > 0:
+            pl.semaphore_wait(round_sem.at[r - 1], 1)
+        if r < 7:
+            pl.semaphore_signal(
+                round_sem.at[r], inc=1, device_id=device(flip((16, 32, 4, 8, 2, 1, 64)[r])), device_id_type=MESH
+            )
+
     barrier = pltpu.get_barrier_semaphore()
     greeted = [device(flip(bit)) for bit in (2, 8, 32, 64)] + [above, below]
     for step in (1, 3):
@@ -243,6 +251,7 @@
     pl.semaphore_wait(barrier, len(greeted))
     fetch_z(0)
     fetch_z(1)
+    greet(0)
     perm[0] = one_hot(True)
     perm[1] = one_hot(False)
     own_frames.wait()
@@ -271,19 +280,13 @@
                 qkv_s[every, 2 * HALF + c : 2 * HALF + c + 128],
             )
 
-    def rounds(low, high):
-        for r in range(low, high):
-            pl.semaphore_signal(
-                round_sem.at[r], inc=1, device_id=device(flip((16, 32, 4, 8, 2, 1, 64)[r])), device_id_type=MESH
-            )
-            pl.semaphore_wait(round_sem.at[r], 1)
-
+    greet(1)
     spatial_qkv(m)
     fetch_ring(0)
     fetch_ring(1)
     fetch_z(2)
     fetch_z(3)
-    rounds(0, 2)
+    greet(2)
 
     @pl.loop(0, 4)
     def _(f):
@@ -293,7 +296,15 @@
             fetch_far(1)
             fetch_z(4)
             fetch_z(5)
-            rounds(2, 4)
+            greet(4)
+
+        @pl.when(f == 1)
+        def _():
+            greet(3)
+
+        @pl.when(f == 3)
+        def _():
+            greet(5)
 
         spatial_heads(m, f, 0, TOKENS)
 
@@ -301,9 +312,10 @@
     fetch_last(1)
     fetch_ring(2)
     fetch_ring(3)
-    rounds(4, 7)
+    greet(6)
     fetched(0)
     spatial_qkv(1 - m)
+    greet(7)
 
     @pl.loop(0, 2)
     def _(p):
@@ -374,14 +386,14 @@
             for half in range(2):
                 qkv_t[half, rows] = (dot(normal, f2[half]) * scale).astype(BF16)
 
-        @pl.when(p == 0)
-        def _():
-            fetch_far(4)
-            fetch_far(5)
-
         @pl.loop(0, 4)
         def _(t):
-            @pl.when(jnp.logical_and(p == 0, t == 2))
+            @pl.when(jnp.logical_and(p == 0, t == 1))
+            def _():
+                fetch_far(4)
+                fetch_far(5)
+
+            @pl.when(jnp.logical_and(p == 0, t == 3))
             def _():
                 fetch_last(4)
                 fetch_last(5)

time: 106 us -> 102 us (0.962)
  Pallas kernels: 103 us -> 99.6 us
    pallas_call x1, Pallas kernels: 103 us -> 99.6 us  [per_device(): pl.pallas_call(kernel, out_shape=jax.ShapeDtypeStruct((4, 256, D), BF16),...]
where the time goes in v5:
time: 102 us
  Pallas kernels  99.6 us (98%)
  local copies, waits for them, and re-layouts  2.65 us (3%)
    pallas_call x1, Pallas kernels, per_device(): pl.pallas_call(kernel, out_shape=jax.ShapeDtypeStruct((4, 256, D), BF16),...  99.6 us
    unnamed x1, local copies, waits for them, and re-layouts  2.65 us

profile of v5, /device:TPU:1, one launch (start us, length us, event | category | flops | bytes accessed | tf_op | source)
XLA Modules:
  0.0 102.3 jit_solution(9268285976051960657)
XLA Ops:
  0.0 99.6 %shard_map.100 = bf16[4,256,768]{2,1,0:T(8,128)(2,1)} custom-call(bf16[8,256,768]{2,1,0:T(8,128)(2,1)} %clip.1, f32[768]{0:T(1024)} %gain_s.1, f32[768]{0:T(1024)} %gain_t.1, f32[768]{0:T(1024)} %gain_m.1, bf16[3,768,384]{2,1,0:T(8,128)(2,1)} %bitcast.2, bf16[384,768]{1,0:T(8,128)(2,1)} %w1.1, bf16[3,768,384]{2,1,0:T(8,128)(2,1)} %bitcast.3, ...), custom_call_target="tpu_custom_call" | custom-call | flops 22000001024 | bytes 13000000 | tf_op jit(solution)/shard_map/pallas_call | solution.py:466
  99.6 2.7 %copy.12 = bf16[4,256,768]{2,1,0:T(8,128)(2,1)} copy(bf16[4,256,768]{2,1,0:T(8,128)(2,1)} %shard_map.100) | data formatting | bytes 3145728

commit v6 on v5

--- a/solution.py
+++ b/solution.py
@@ -293,7 +293,6 @@
         @pl.when(f == 2)
         def _():
             fetch_far(0)
-            fetch_far(1)
             fetch_z(4)
             fetch_z(5)
             greet(4)
@@ -309,12 +308,13 @@
         spatial_heads(m, f, 0, TOKENS)
 
     fetch_last(0)
-    fetch_last(1)
+    fetch_far(1)
     fetch_ring(2)
-    fetch_ring(3)
     greet(6)
     fetched(0)
     spatial_qkv(1 - m)
+    fetch_last(1)
+    fetch_ring(3)
     greet(7)
 
     @pl.loop(0, 2)

time: 102 us -> 104 us (1.020)
  Pallas kernels: 99.6 us -> 101 us
    pallas_call x1, Pallas kernels: 99.6 us -> 101 us  [per_device(): pl.pallas_call(kernel, out_shape=jax.ShapeDtypeStruct((4, 256, D), BF16),...]
where the time goes in v6:
time: 104 us
  Pallas kernels  101 us (97%)
  local copies, waits for them, and re-layouts  2.65 us (3%)
    pallas_call x1, Pallas kernels, per_device(): pl.pallas_call(kernel, out_shape=jax.ShapeDtypeStruct((4, 256, D), BF16),...  101 us
    unnamed x1, local copies, waits for them, and re-layouts  2.65 us

profile of v6, /device:TPU:1, one launch (start us, length us, event | category | flops | bytes accessed | tf_op | source)
XLA Modules:
  0.0 104.1 jit_solution(2653933887614817615)
XLA Ops:
  0.0 101.4 %shard_map.100 = bf16[4,256,768]{2,1,0:T(8,128)(2,1)} custom-call(bf16[8,256,768]{2,1,0:T(8,128)(2,1)} %clip.1, f32[768]{0:T(1024)} %gain_s.1, f32[768]{0:T(1024)} %gain_t.1, f32[768]{0:T(1024)} %gain_m.1, bf16[3,768,384]{2,1,0:T(8,128)(2,1)} %bitcast.2, bf16[384,768]{1,0:T(8,128)(2,1)} %w1.1, bf16[3,768,384]{2,1,0:T(8,128)(2,1)} %bitcast.3, ...), custom_call_target="tpu_custom_call" | custom-call | flops 22000001024 | bytes 13000000 | tf_op jit(solution)/shard_map/pallas_call | solution.py:466
  101.4 2.7 %copy.12 = bf16[4,256,768]{2,1,0:T(8,128)(2,1)} copy(bf16[4,256,768]{2,1,0:T(8,128)(2,1)} %shard_map.100) | data formatting | bytes 3145728
